TPU v7x, 32 devices: a whole 2x2x4 slice. The times are simulated.
32 devices in a mesh: row: 4 (over z), col: 8 (over y, x, core).
Axes of the slice: x: 2, y: 2, z: 4, core: 2. Of those that a mesh axis runs over, the one named last changes fastest.
Arguments:
- tokens: bfloat16 [1024, 4096], P('row', 'col'), may hold values from -6 to 6
- norm_gain: float32 [4096], replicated, may hold values from 0.1 to 1.9
- expert_ids: int32 [1024, 2], P('row'), may hold values from 0 to 7, all different within a row; in each aligned block of 256 rows (0 to 255, 256 to 511, ...) at most 128 rows name the same one
- gate_weights: float32 [1024, 2], P('row'), may hold values from 0.1 to 1
- w_gate: bfloat16 [8, 4096, 14336], P('row', None, 'col'), may hold values from -0.09375 to 0.09375
- w_up: bfloat16 [8, 4096, 14336], P('row', None, 'col'), may hold values from -0.09375 to 0.09375
- w_down: bfloat16 [8, 14336, 4096], P('row', 'col'), may hold values from -0.046875 to 0.046875
Outputs:
- layer_output: bfloat16 [1024, 4096], P('row', 'col')
Inputs may be any that keep to these rules, and one draw needn't show every extreme that they name: `expert_ids`: the 2 experts of a token differ. In each aligned block of 256 tokens no expert is chosen by more than 128 tokens, a bound that some block reaches.
All inputs are finite; a program needn't handle non-finite values.
Results may differ from a plain program's by a relative error of at most 0.0043.
Values may be sent and summed in bfloat16 or wider, within the bound.
No kernel may reach another device: no remote copies, remote signals or barrier semaphores. Data moves between devices by JAX's collectives and lax.ppermute only.
A program may use at most 192 MiB of HBM per device.

v0:
```python
import jax
import jax.numpy as jnp
from jax import lax
from jax.sharding import PartitionSpec as P

EXPERTS = 8
CAP = 128


def normalize(rows, norm_gain):
    values = rows.astype(jnp.float32)
    inverse_norm = lax.rsqrt(jnp.mean(values * values, axis=-1, keepdims=True) + 1e-05)
    return (values * inverse_norm * norm_gain).astype(jnp.bfloat16)


def route_tables(expert_ids, expert_count, capacity):
    token_count = expert_ids.shape[0]
    flat_ids = expert_ids.reshape(-1)
    expert_range = jnp.arange(expert_count, dtype=jnp.int32)
    expert_hits = (flat_ids[:, None] == expert_range[None, :]).astype(jnp.int32)
    earlier = jnp.cumsum(expert_hits, axis=0) - expert_hits
    ranks = jnp.sum(earlier * expert_hits, axis=1)
    slot_index = (flat_ids * capacity + ranks).reshape(token_count, -1)
    slot_ids = jnp.arange(expert_count * capacity, dtype=jnp.int32)
    matches = (slot_index[:, :, None] == slot_ids[None, None, :]).astype(jnp.float32)
    picker = jnp.sum(matches, axis=1)
    return (picker.astype(jnp.bfloat16), slot_index)


def combine_rows(slot_rows, slot_index, gate_weights):
    picked = slot_rows[slot_index]
    return jnp.sum(picked * gate_weights[:, :, None], axis=1)


def run_experts(normed, gate_block, up_block, down_block):
    local_count = gate_block.shape[0]
    sources = normed.shape[0] // local_count
    grouped = normed.reshape(sources, local_count, normed.shape[1], normed.shape[2])
    gate_part = jnp.einsum(
        "slcd,ldf->slcf", grouped, gate_block, preferred_element_type=jnp.float32
    )
    up_part = jnp.einsum("slcd,ldf->slcf", grouped, up_block, preferred_element_type=jnp.float32)
    hidden = (jax.nn.silu(gate_part) * up_part).astype(jnp.bfloat16)
    outputs = jnp.einsum("slcf,lfd->slcd", hidden, down_block, preferred_element_type=jnp.float32)
    return outputs.reshape(normed.shape[0], normed.shape[1], down_block.shape[2])


def body(tokens, norm_gain, expert_ids, gate_weights, w_gate, w_up, w_down):
    picker, slot_index = route_tables(expert_ids, EXPERTS, CAP)
    packed = jnp.einsum("ts,td->sd", picker, tokens, preferred_element_type=jnp.float32).astype(
        jnp.bfloat16
    )
    packed = packed.reshape(EXPERTS, CAP, tokens.shape[1])
    arrived = lax.all_to_all(packed, "row", split_axis=0, concat_axis=0, tiled=True)
    widened = lax.all_gather(arrived, "col", axis=2, tiled=True)
    normed = normalize(widened, norm_gain)
    outputs = run_experts(normed, w_gate, w_up, w_down)
    shares = lax.psum_scatter(outputs, "col", scatter_dimension=2, tiled=True)
    returned = lax.all_to_all(shares, "row", split_axis=0, concat_axis=0, tiled=True)
    mixed = combine_rows(returned.reshape(-1, shares.shape[2]), slot_index, gate_weights)
    return (tokens.astype(jnp.float32) + mixed).astype(jnp.bfloat16)


def solution(mesh):
    placed = (
        P("row", "col"),
        P(),
        P("row", None),
        P("row", None),
        P("row", None, "col"),
        P("row", None, "col"),
        P("row", "col", None),
    )
    return jax.shard_map(
        body, mesh=mesh, in_specs=placed, out_specs=P("row", "col"), check_vma=False
    )
```

profile of v0, /device:TPU:0, one launch (start us, length us, event | category | flops | bytes accessed | tf_op | source)
XLA Modules:
  0.0 379.3 jit_solution(16247418307875765036)
XLA Ops:
  6.5 0.0 copy-start.1
  6.5 0.0 all-gather.2.cloned.1.call-start
  6.5 0.8 copy.26
  7.4 0.1 eq.42
  7.5 0.1 eq.38
  7.7 1.1 reduce-window.6
  8.8 0.2 slice_reduce_fusion
  9.1 0.1 fusion.24
  9.2 0.1 reduce_sum.39
  9.3 0.1 copy.28
  9.4 0.7 compare_select_fusion
  10.1 0.3 convert_reduce_fusion
  10.4 1.4 convolution_convert_fusion
  11.8 31.9 %all_to_all.10 = bf16[8,128,512]{2,1,0:T(8,128)(2,1)} all-to-all(bf16[8,128,512]{2,1,0:T(8,128)(2,1)S(1)} %bitcast.57), channel_id=1, replica_groups=mesh['row'=4,'col'=8] {'row'}, dimensions={0} | all-to-all | bytes 2097152 | tf_op jit(solution)/shard_map/all_to_all | solution.py:54
  43.7 0.0 all-gather.2.cloned.1.call-update
  43.8 0.0 reduce-scatter.2.cloned.1.call-start
  43.8 55.2 %all-gather.2.cloned.1.call-done = bf16[8,128,4096]{2,1,0:T(8,128)(2,1)} async-done(((bf16[8,128,512]{2,1,0:T(8,128)(2,1)}), bf16[8,128,4096]{2,1,0:T(8,128)(2,1)}) %all-gather.2.cloned.1.call-update) | async-done | bytes 8388624 | tf_op jit(solution)/shard_map/all_gather | solution.py:55
  99.0 5.1 %fusion.6 = f32[8,128]{1,0:T(8,128)S(1)} fusion(bf16[8,128,4096]{2,1,0:T(8,128)(2,1)} %all-gather.2.cloned.1.call-done), kind=kLoop, calls=%fused_computation.9 | loop fusion | flops 12581888 | bytes 8392704 | tf_op jit(solution)/shard_map/reduce_sum | solution.py:12
  104.1 0.0 copy-done.1
  104.1 10.3 %fusion.8 = bf16[8,128,4096]{2,1,0:T(8,128)(2,1)} fusion(bf16[8,128,4096]{2,1,0:T(8,128)(2,1)} %all-gather.2.cloned.1.call-done, f32[4096]{0:T(1024)S(1)} %copy-done.1, f32[8,128]{1,0:T(8,128)S(1)} %add_rsqrt_fusion), kind=kLoop, calls=%fused_computation.11 | loop fusion | flops 16777216 | bytes 16797696 | tf_op jit(solution)/shard_map/convert_element_type | solution.py:13
  114.4 23.8 %fusion.4 = f32[2,4,128,1792]{3,2,1,0:T(8,128)} fusion(bf16[2,4096,1792]{2,1,0:T(8,128)(2,1)} %param.11, bf16[4,2,128,4096]{3,2,1,0:T(8,128)(2,1)} %bitcast.55), kind=kOutput, calls=%fused_computation.5 | convolution fusion | flops 15032385536 | bytes 45088768 | tf_op jit(solution)/shard_map/slcd,ldf->slcf/dot_general | solution.py:39
  138.2 24.4 %fusion.14 = bf16[4,2,128,1792]{3,2,0,1:T(8,128)(2,1)} fusion(f32[2,4,128,1792]{3,2,1,0:T(8,128)} %fusion.4, bf16[2,4096,1792]{2,1,0:T(8,128)(2,1)} %param.12, bf16[4,2,128,4096]{3,2,1,0:T(8,128)(2,1)} %bitcast.56), kind=kOutput, calls=%fused_computation.16 | convolution fusion | flops 15043395584 | bytes 48758784 | tf_op jit(solution)/shard_map/slcd,ldf->slcf/dot_general | solution.py:42
  162.6 25.0 %fusion.9 = f32[4,2,128,4096]{3,2,0,1:T(8,128)} fusion(bf16[4,2,128,1792]{3,2,0,1:T(8,128)(2,1)} %fusion.14, bf16[2,1792,4096]{2,1,0:T(8,128)(2,1)} %param.13), kind=kOutput, calls=%fused_computation.12 | convolution fusion | flops 15032385536 | bytes 49807360 | tf_op jit(solution)/shard_map/slcf,lfd->slcd/dot_general | solution.py:44
  187.6 11.6 %copy.31 = f32[4,2,128,4096]{3,2,1,0:T(8,128)} copy(f32[4,2,128,4096]{3,2,0,1:T(8,128)} %fusion.9) | data formatting | bytes 33554432 | tf_op jit(solution)/shard_map/slcf,lfd->slcd/transpose | solution.py:44
  199.2 0.0 copy-start.2
  199.2 0.0 reduce-scatter.2.cloned.1.call-update
  199.2 0.0 copy-start
  199.2 116.1 %reduce-scatter.2.cloned.1.call-done = f32[8,128,512]{2,1,0:T(8,128)} async-done(((f32[8,128,4096]{2,1,0:T(8,128)}), f32[8,128,512]{2,1,0:T(8,128)}) %reduce-scatter.2.cloned.1.call-update) | async-done | bytes 2097168 | tf_op jit(solution)/shard_map/reduce_scatter | solution.py:58
  315.3 4.6 %all-to-all-start.1 = ((f32[8,128,512]{2,1,0:T(8,128)}), f32[8,128,512]{2,1,0:T(8,128)S(1)}, u32[]{:S(2)}, u32[]{:S(2)}) async-start(f32[8,128,512]{2,1,0:T(8,128)} %reduce-scatter.2.cloned.1.call-done), calls=%async_computation.2 | async-start | bytes 4194304 | tf_op jit(solution)/shard_map/all_to_all | solution.py:59
  319.9 0.1 copy.32
  320.1 0.1 reshape.55
  320.2 0.0 copy-done.2
  320.2 0.1 copy.33
  320.4 47.7 %all-to-all-done.1 = f32[8,128,512]{2,1,0:T(8,128)S(1)} async-done(((f32[8,128,512]{2,1,0:T(8,128)}), f32[8,128,512]{2,1,0:T(8,128)S(1)}, u32[]{:S(2)}, u32[]{:S(2)}) %all-to-all-start.1) | async-done | bytes 2097184 | tf_op jit(solution)/shard_map/all_to_all | solution.py:59
  368.1 1.6 gather_fusion
  369.7 0.6 reshape.54
  370.3 1.3 multiply_reduce_fusion
  371.7 0.0 copy-done
  371.7 0.8 add_convert_fusion
  (5 shorter events, 0.1 us)
Async XLA Ops:
  6.5 97.5 %copy-start.1 = (f32[4096]{0:T(1024)S(1)}, f32[4096]{0:T(1024)}, u32[]{:S(2)}) copy-start(f32[4096]{0:T(1024)} %param.8) | copy-start | bytes 49156
  6.5 92.4 %all-gather.2.cloned.1.call-start = ((), (), s32[]{:S(2)}) async-start(), calls=%async_computation.3 | async-start | bytes 9437184 | tf_op jit(solution)/shard_map/all_gather | solution.py:55
  43.8 271.6 %reduce-scatter.2.cloned.1.call-start = ((), (), s32[]{:S(2)}) async-start(), calls=%async_computation.4 | async-start | bytes 18874368 | tf_op jit(solution)/shard_map/reduce_scatter | solution.py:58
  199.2 121.0 %copy-start.2 = (f32[256,2]{0,1:T(2,128)S(1)}, f32[256,2]{0,1:T(2,128)}, u32[]{:S(2)}) copy-start(f32[256,2]{0,1:T(2,128)} %param.10) | copy-start | bytes 6148
  199.2 172.5 %copy-start = (bf16[256,512]{1,0:T(8,128)(2,1)S(1)}, bf16[256,512]{1,0:T(8,128)(2,1)}, u32[]{:S(2)}) copy-start(bf16[256,512]{1,0:T(8,128)(2,1)} %param.7) | copy-start | bytes 786436
  315.3 52.7 %all-to-all-start.1 = ((f32[8,128,512]{2,1,0:T(8,128)}), f32[8,128,512]{2,1,0:T(8,128)S(1)}, u32[]{:S(2)}, u32[]{:S(2)}) async-start(f32[8,128,512]{2,1,0:T(8,128)} %reduce-scatter.2.cloned.1.call-done), calls=%async_computation.2 | async-start | bytes 4194304 | tf_op jit(solution)/shard_map/all_to_all | solution.py:59
Sparse Core Ops, SparseCore 0:
  43.9 55.0 all-gather.1
  199.3 115.9 reduce-scatter.1
where the time goes:
time: 380 us; the launch traced here: 379 us
  waiting for transfers between devices  219 us (58%)
  matrix products  74.6 us (20%)
  blocking collectives  31.9 us (8%)
  other arithmetic  19.8 us (5%)
  local copies, waits for them, and re-layouts  15.8 us (4%)
  between operations  13.5 us (4%)
  starting transfers between devices  4.62 us (1%)
    reduce_scatter x1, waiting for transfers between devices, body(): shares = lax.psum_scatter(outputs, 'col', scatter_dimension=2, tiled=True)  116 us
    all_gather x1, waiting for transfers between devices, body(): widened = lax.all_gather(arrived, 'col', axis=2, tiled=True)  55.2 us
    all_to_all x1, waiting for transfers between devices, body(): lax.all_to_all(shares, 'row', split_axis=0, concat_axis=0, tiled=True)  47.7 us
    all_to_all x1, blocking collectives, body(): lax.all_to_all(packed, 'row', split_axis=0, concat_axis=0, tiled=True)  31.9 us
    dot_general x1, matrix products, run_experts(): jnp.einsum('slcf,lfd->slcd', hidden, down_block, preferred_element_type=j...  25 us
    dot_general x1, matrix products, run_experts(): jnp.einsum('slcd,ldf->slcf', grouped, up_block, preferred_element_type=jn...  24.4 us
    dot_general x1, matrix products, run_experts(): jnp.einsum('slcd,ldf->slcf', grouped, gate_block, preferred_element_type=...  23.8 us
    transpose x1, local copies, waits for them, and re-layouts, run_experts(): jnp.einsum('slcf,lfd->slcd', hidden, down_block, preferred_element_type=j...  11.6 us
  transfers between devices with their start and end apart: 3, of which 3 were waited for; matrix products, arithmetic and copies ran while one was open for 0% of the time, Pallas kernels for 0%

commit v1 on v0

v1 whole, which is shorter than its diff:
```python
import functools
import jax
import jax.numpy as jnp
from jax import lax
from jax.experimental import pallas as pl
from jax.experimental.pallas import tpu as pltpu
from jax.sharding import PartitionSpec as P

EXPERTS = 8
CAP = 128
SLOTS = 3
F32 = jnp.float32
BF16 = jnp.bfloat16
VMEM = 64 * 1024 * 1024


def pack_kernel(chosen, base_ref, ids_ref, tokens_ref, *out_refs):
    tokens = tokens_ref.shape[0]
    numbers = lax.broadcasted_iota(jnp.int32, (EXPERTS, tokens), 0)
    ids = jnp.bitwise_xor(ids_ref[...], base_ref[0])
    hit = (numbers == ids[0:1, :]) | (numbers == ids[1:2, :])
    hits = jnp.where(hit, 1.0, 0.0)
    before = lax.broadcasted_iota(jnp.int32, (tokens, tokens), 0)
    after = lax.broadcasted_iota(jnp.int32, (tokens, tokens), 1)
    upper = jnp.where(before < after, 1.0, 0.0).astype(BF16)
    ranks = jnp.dot(hits.astype(BF16), upper, preferred_element_type=F32)
    ranks = jnp.where(hit, ranks, -1.0)
    slots = lax.broadcasted_iota(jnp.int32, (CAP, tokens), 0).astype(F32)
    for out_ref, experts in zip(out_refs, chosen):
        for index, expert in enumerate(experts):
            picker = jnp.where(slots == ranks[expert : expert + 1, :], 1.0, 0.0).astype(BF16)
            rows = jnp.dot(picker, tokens_ref[...], preferred_element_type=F32)
            out_ref[index] = rows.astype(BF16)


def pack(chosen, base, ids, tokens):
    width = tokens.shape[1]
    vmem = pl.BlockSpec(memory_space=pltpu.VMEM)
    return pl.pallas_call(
        functools.partial(pack_kernel, chosen),
        out_shape=[jax.ShapeDtypeStruct((len(c), CAP, width), BF16) for c in chosen],
        in_specs=[pl.BlockSpec(memory_space=pltpu.SMEM), vmem, vmem],
        out_specs=[vmem] * len(chosen),
        compiler_params=pltpu.CompilerParams(vmem_limit_bytes=VMEM),
        name="pack",
    )(base, ids, tokens)


def stack_kernel(layout, count, *refs):
    sources, out_refs = refs[:count], refs[-len(layout) :]
    for out_ref, parts in zip(out_refs, layout):
        for index, (source, at) in enumerate(parts):
            out_ref[index] = sources[source][at]


def stack(layout, sources, token=None):
    tokens = () if token is None else (token,)
    vmem = pl.BlockSpec(memory_space=pltpu.VMEM)
    block = sources[0].shape[1:]
    return pl.pallas_call(
        functools.partial(stack_kernel, layout, len(sources)),
        out_shape=[jax.ShapeDtypeStruct((len(parts),) + block, BF16) for parts in layout],
        in_specs=[vmem] * len(sources) + [pl.BlockSpec(memory_space=pltpu.SMEM)] * len(tokens),
        out_specs=[vmem] * len(layout),
        compiler_params=pltpu.CompilerParams(vmem_limit_bytes=VMEM),
        name="stack",
    )(*sources, *tokens)


def combine_kernel(experts, base_ref, ids_ref, weights_ref, start_ref, *refs):
    slot_refs, out_ref = refs[:-1], refs[-1]
    tokens = start_ref.shape[0]
    ids = jnp.bitwise_xor(ids_ref[...], base_ref[0]).astype(F32)
    filler = jnp.zeros((4, tokens), F32)
    columns = jnp.transpose(jnp.concatenate([ids, weights_ref[...], filler], axis=0))
    lanes = lax.broadcasted_iota(jnp.int32, (tokens, 128), 1).astype(F32)
    first, second = columns[:, 0:1], columns[:, 1:2]
    hits = jnp.where((lanes == first) | (lanes == second), 1.0, 0.0)
    row = lax.broadcasted_iota(jnp.int32, (tokens, tokens), 0)
    column = lax.broadcasted_iota(jnp.int32, (tokens, tokens), 1)
    lower = jnp.where(column < row, 1.0, 0.0).astype(BF16)
    ranks = jnp.dot(lower, hits.astype(BF16), preferred_element_type=F32)
    total = start_ref[...].astype(F32)
    for choice, chosen in enumerate((first, second)):
        rank = jnp.sum(jnp.where(lanes == chosen, ranks, 0.0), axis=1, keepdims=True)
        matches = jnp.where(lanes == rank, 1.0, 0.0)
        picked = jnp.zeros(total.shape, F32)
        for expert, slot_ref in zip(experts, slot_refs):
            picker = jnp.where(chosen == expert, matches, 0.0).astype(BF16)
            picked += jnp.dot(picker, slot_ref[...], preferred_element_type=F32)
        total += picked * columns[:, 2 + choice : 3 + choice]
    out_ref[...] = total.astype(out_ref.dtype)


def combine(experts, base, ids, gate_weights, start, slots, kind):
    vmem = pl.BlockSpec(memory_space=pltpu.VMEM)
    return pl.pallas_call(
        functools.partial(combine_kernel, experts),
        out_shape=jax.ShapeDtypeStruct(start.shape, kind),
        in_specs=[pl.BlockSpec(memory_space=pltpu.SMEM)] + [vmem] * (3 + len(slots)),
        out_specs=vmem,
        compiler_params=pltpu.CompilerParams(vmem_limit_bytes=VMEM),
        name="combine",
    )(base, ids, gate_weights, start, *slots)


def up_kernel(expert, blocks, cols, places, place_ref, gain_ref, *refs):
    count = blocks * cols
    pieces = refs[:count]
    w_gate, w_up, w_down = refs[count : count + 3]
    (send_out, early_out, hidden_out, done_out, raw, scaled, ups, downs, hidden, staged, total, squares) = refs[-18:-6]
    x_sem, gate_sem, up_sem, down_sem, out_sem, hidden_sem = refs[-6:]
    slots, features = ups.shape[0], ups.shape[1]
    tile, units, width = ups.shape[2] // 2, hidden.shape[1], raw.shape[2]
    tiles, half = units // tile, cols // 2
    place = place_ref[0]
    done_out[0] = place

    def up_copies(index):
        slot = lax.rem(index, slots)
        columns = pl.ds(pl.multiple_of(index * tile, tile), tile)
        return (
            pltpu.make_async_copy(
                w_gate.at[expert, :, columns], ups.at[slot, :, pl.ds(0, tile)], gate_sem.at[slot]
            ),
            pltpu.make_async_copy(
                w_up.at[expert, :, columns], ups.at[slot, :, pl.ds(tile, tile)], up_sem.at[slot]
            ),
        )

    def down_copy(index):
        core, at = (1, index) if index < half else (0, index - half)
        return down_piece(expert, w_down, downs, down_sem, place, index, at, core)

    def piece_copies(relative):
        copies = []
        for block in range(blocks):
            number = block * cols + relative
            piece, at = pieces[number], places[number]
            if len(piece.shape) == 4:
                source = piece.at[jnp.bitwise_xor(place, relative), at]
            else:
                source = piece.at[at]
            target = raw.at[relative, pl.ds(block * CAP, CAP), :]
            copies.append(pltpu.make_async_copy(source, target, x_sem.at[number]))
        return copies

    for relative in range(cols):
        for copy in piece_copies(relative):
            copy.start()
    for copy in up_copies(0):
        copy.start()
    for relative in range(cols):
        for copy in piece_copies(relative):
            copy.wait()
        if relative == 0:
            for copy in up_copies(0):
                copy.wait()
            for index in range(1, slots):
                for copy in up_copies(index):
                    copy.start()
        owner = jnp.bitwise_xor(place, relative)
        at = pl.ds(pl.multiple_of(owner * width, width), width)
        values = raw[relative].astype(F32)
        square = values * values
        part = square[:, 0:128]
        for lane in range(128, width, 128):
            part += square[:, lane : lane + 128]
        share = (values * gain_ref[owner]).astype(BF16)
        scaled[:, at] = share
        product = jnp.dot(share, ups[0, at, :], preferred_element_type=F32)
        if relative == 0:
            squares[...] = part
            total[...] = product
        else:
            squares[...] += part
            total[...] += product
    mean = jnp.sum(squares[...], axis=1, keepdims=True) * (1.0 / features)
    squares[...] = jnp.broadcast_to(lax.rsqrt(mean + 1e-05), squares.shape)

    def activate(both, columns):
        inverse = squares[:, 0:1]
        gate, up = both[:, :tile] * inverse, both[:, tile:] * inverse
        hidden[:, columns] = (gate / (1.0 + jnp.exp(-gate)) * up).astype(BF16)

    activate(total[...], pl.ds(0, tile))

    @pl.loop(1, tiles)
    def _(index):
        for copy in up_copies(index):
            copy.wait()

        @pl.when(index + slots - 1 < tiles)
        def _():
            for copy in up_copies(index + slots - 1):
                copy.start()

        for step in range(half + half // 2):

            @pl.when(index == tiles - slots + 1 + step * (slots - 1) // (half + half // 2))
            def _():
                down_copy(step).start()

        both = jnp.dot(scaled[...], ups[lax.rem(index, slots)], preferred_element_type=F32)
        activate(both, pl.ds(pl.multiple_of(index * tile, tile), tile))

    hidden_copy = pltpu.make_async_copy(hidden, hidden_out, hidden_sem)
    hidden_copy.start()
    targets = [send_out.at[index] for index in range(half)]
    targets += [early_out.at[index] for index in range(half // 2)]
    finish_down(targets, hidden, downs, staged, down_copy, out_sem)
    hidden_copy.wait()


def down_piece(expert, w_down, downs, down_sem, place, slot, index, core):
    width = downs.shape[2] // 2
    owner = jnp.bitwise_xor(place, 2 * index + core)
    return pltpu.make_async_copy(
        w_down.at[expert, :, pl.ds(pl.multiple_of(owner * width, width), width)],
        downs.at[slot // 2, :, pl.ds(slot % 2 * width, width)],
        down_sem.at[slot],
    )


def finish_down(targets, hidden, downs, staged, down_copy, out_sem):
    outs = []
    width = downs.shape[2] // 2
    for index in range(0, len(targets), 2):
        down_copy(index).wait()
        down_copy(index + 1).wait()
        both = jnp.dot(hidden[...], downs[index // 2], preferred_element_type=F32).astype(BF16)
        for at in (index, index + 1):
            start = (at - index) * width
            staged[at] = both[:, start : start + width]
            outs.append(pltpu.make_async_copy(staged.at[at], targets[at], out_sem.at[at]))
            outs[-1].start()
    for out in outs:
        out.wait()


def down_kernel(expert, count, place_ref, hidden_ref, w_down, *refs):
    terms = refs[:count]
    hidden, downs, staged, down_sem, out_sem, hidden_sem = refs[-6:]
    late = staged.shape[0]

    def down_copy(index):
        return down_piece(expert, w_down, downs, down_sem, place_ref[0], index, late + index, 0)

    hidden_copy = pltpu.make_async_copy(hidden_ref, hidden, hidden_sem)
    hidden_copy.start()
    if count:
        late_out, low_out, high_out, held, summed, term_sem, sum_sem = refs[-13:-6]
        copies = [
            pltpu.make_async_copy(terms[index], held.at[index], term_sem.at[index])
            for index in range(count)
        ]
        for copy in copies:
            copy.start()
    else:
        late_out = refs[-7]
    for index in range(late):
        down_copy(index).start()
    outs = []
    if count:
        for copy in copies:
            copy.wait()
        total = held[0].astype(F32)
        for index in range(1, count):
            total += held[index].astype(F32)
        summed[...] = total.astype(BF16)
        for index, out_ref in enumerate((low_out, high_out)):
            rows = pl.ds(index * CAP, CAP)
            outs.append(pltpu.make_async_copy(summed.at[rows], out_ref, sum_sem.at[index]))
            outs[-1].start()
    hidden_copy.wait()
    targets = [late_out.at[index] for index in range(late)]
    finish_down(targets, hidden, downs, staged, down_copy, out_sem)
    for out in outs:
        out.wait()


def expand(expert, pieces, place, norm_gain, w_gate, w_up, w_down, after=()):
    blocks, cols = len(pieces), len(pieces[0])
    features, units = w_gate.shape[1], w_gate.shape[2]
    width, rows, half = features // cols, blocks * CAP, cols // 2
    tile = 256 if units % 256 == 0 else 128
    anywhere = pl.BlockSpec(memory_space=pl.ANY)
    flat = [array for block in pieces for array, _ in block]
    places = [index for block in pieces for _, index in block]
    downs = half + half // 2
    weights = 2 * features * units + downs * units * width
    return pl.pallas_call(
        functools.partial(up_kernel, expert, blocks, cols, places),
        out_shape=[
            jax.ShapeDtypeStruct((half, rows, width), BF16),
            jax.ShapeDtypeStruct((half // 2, rows, width), BF16),
            jax.ShapeDtypeStruct((rows, units), BF16),
            jax.ShapeDtypeStruct((1,), jnp.int32),
        ],
        in_specs=[
            pl.BlockSpec(memory_space=pltpu.SMEM),
            pl.BlockSpec(memory_space=pltpu.VMEM),
        ]
        + [anywhere] * (len(flat) + 3 + len(after)),
        out_specs=[anywhere, anywhere, anywhere, pl.BlockSpec(memory_space=pltpu.SMEM)],
        scratch_shapes=[
            pltpu.VMEM((cols, rows, width), BF16),
            pltpu.VMEM((rows, features), BF16),
            pltpu.VMEM((SLOTS, features, 2 * tile), BF16),
            pltpu.VMEM((downs // 2, units, 2 * width), BF16),
            pltpu.VMEM((rows, units), BF16),
            pltpu.VMEM((downs, rows, width), BF16),
            pltpu.VMEM((rows, 2 * tile), F32),
            pltpu.VMEM((rows, 128), F32),
            pltpu.SemaphoreType.DMA((len(flat),)),
            pltpu.SemaphoreType.DMA((SLOTS,)),
            pltpu.SemaphoreType.DMA((SLOTS,)),
            pltpu.SemaphoreType.DMA((downs,)),
            pltpu.SemaphoreType.DMA((downs,)),
            pltpu.SemaphoreType.DMA,
        ],
        compiler_params=pltpu.CompilerParams(vmem_limit_bytes=VMEM),
        cost_estimate=pl.CostEstimate(
            flops=2 * rows * weights, bytes_accessed=2 * weights, transcendentals=rows * units
        ),
        name="expand",
    )(place, norm_gain.reshape(cols, 1, width), *flat, w_gate, w_up, w_down, *after)


def contract(expert, hidden, cols, place, w_down, terms=(), after=()):
    rows, units = hidden.shape
    width, late, count = w_down.shape[2] // cols, cols // 4, len(terms)
    anywhere = pl.BlockSpec(memory_space=pl.ANY)
    weights = units * width * late
    block = jax.ShapeDtypeStruct((CAP, width), BF16)
    side = [
        pltpu.VMEM((count, rows, width), BF16),
        pltpu.VMEM((rows, width), BF16),
        pltpu.SemaphoreType.DMA((count,)),
        pltpu.SemaphoreType.DMA((2,)),
    ]
    out_shape = [jax.ShapeDtypeStruct((late, rows, width), BF16)] + [block, block] * bool(count)
    return pl.pallas_call(
        functools.partial(down_kernel, expert, count),
        out_shape=out_shape,
        in_specs=[pl.BlockSpec(memory_space=pltpu.SMEM)] + [anywhere] * (2 + count + len(after)),
        out_specs=[anywhere] * len(out_shape),
        scratch_shapes=side * bool(count)
        + [
            pltpu.VMEM((rows, units), BF16),
            pltpu.VMEM((late // 2, units, 2 * width), BF16),
            pltpu.VMEM((late, rows, width), BF16),
            pltpu.SemaphoreType.DMA((late,)),
            pltpu.SemaphoreType.DMA((late,)),
            pltpu.SemaphoreType.DMA,
        ],
        compiler_params=pltpu.CompilerParams(vmem_limit_bytes=VMEM),
        cost_estimate=pl.CostEstimate(
            flops=128 * rows * weights, bytes_accessed=128 * weights, transcendentals=0
        ),
        name="contract",
    )(place, hidden, w_down, *terms, *after)


def pair_kernel(early_ref, late_ref, other_ref, *refs):
    half = other_ref.shape[0]
    out_refs = refs[:half]
    mine, other, staged, mine_sem, other_sem, out_sem = refs[half:]
    copies = []
    for index in range(half):
        source, at = (early_ref, index) if index < half // 2 else (late_ref, index - half // 2)
        copies.append(
            (
                pltpu.make_async_copy(source.at[at], mine.at[index], mine_sem.at[index]),
                pltpu.make_async_copy(other_ref.at[index], other.at[index], other_sem.at[index]),
            )
        )
    for ours, theirs in copies:
        ours.start()
        theirs.start()
    outs = []
    for index in range(half):
        for copy in copies[index]:
            copy.wait()
        both = mine[index].astype(F32) + other[index].astype(F32)
        staged[index] = both.astype(BF16)
        outs.append(pltpu.make_async_copy(staged.at[index], out_refs[index], out_sem.at[index]))
        outs[-1].start()
    for out in outs:
        out.wait()


def pair_sums(early, late, other):
    half, block = other.shape[0], other.shape[1:]
    anywhere = pl.BlockSpec(memory_space=pl.ANY)
    return pl.pallas_call(
        pair_kernel,
        out_shape=[jax.ShapeDtypeStruct(block, BF16)] * half,
        in_specs=[anywhere] * 3,
        out_specs=[anywhere] * half,
        scratch_shapes=[pltpu.VMEM(other.shape, BF16)] * 3 + [pltpu.SemaphoreType.DMA((half,))] * 3,
        compiler_params=pltpu.CompilerParams(vmem_limit_bytes=VMEM),
        name="pair_sums",
    )(early, late, other)


def add_kernel(count, *refs):
    terms, out_refs = refs[:count], refs[-2:]
    total = terms[0][...].astype(F32)
    for term in terms[1:]:
        total += term[...].astype(F32)
    for index, out_ref in enumerate(out_refs):
        out_ref[...] = total[index * CAP : (index + 1) * CAP].astype(BF16)


def add(terms):
    vmem = pl.BlockSpec(memory_space=pltpu.VMEM)
    block = jax.ShapeDtypeStruct((CAP, terms[0].shape[1]), BF16)
    return pl.pallas_call(
        functools.partial(add_kernel, len(terms)),
        out_shape=[block, block],
        in_specs=[vmem] * len(terms),
        out_specs=[vmem, vmem],
        compiler_params=pltpu.CompilerParams(vmem_limit_bytes=VMEM),
        name="add",
    )(*terms)


def body(rows, cols, tokens, norm_gain, expert_ids, gate_weights, w_gate, w_up, w_down):
    local = EXPERTS // rows
    half = cols // 2
    row, place = lax.axis_index("row"), lax.axis_index("col").reshape(1)

    def along_row(value, relative):
        if relative == 0:
            return value
        return lax.ppermute(value, "row", [(i, i ^ relative) for i in range(rows)])

    def along_col(value, relative):
        if relative == 0:
            return value
        return lax.ppermute(value, "col", [(i, i ^ relative) for i in range(cols)])

    def gather(shares):
        return [along_col(shares, q) for q in range(0, cols, 2)]

    def complete(same_core):
        other_core = [along_col(piece, 1) for piece in same_core]
        return [piece for pair in zip(same_core, other_core) for piece in pair]

    def blocks_of(pieces):
        return [[(p, block) for p in pieces] for block in range(2)]

    base = (row * local).reshape(1)
    ids, token_weights = expert_ids.T, gate_weights.T
    blocks = [(k, k + 1) for k in range(0, rows, 2)]
    experts = range(local)
    chosen = [[k * local + e] for k in range(2) for e in experts]
    chosen += [[k * local + e for e in experts] for k in range(2, rows)]
    packed = pack(chosen, base, ids, tokens)
    own, sent, far = packed[:local], packed[local : 2 * local], packed[2 * local :]
    near = [along_row(share, 1) for share in sent]
    shares = stack([[(0, 0), (1, 0)]], [own[0], near[0]])[0]
    first_pieces = blocks_of(complete(gather(shares)))
    gathered = {}
    stacked = []
    for e in experts[1:]:
        stacked += stack([[(0, 0), (1, 0)]], [own[e], near[e]])
        gathered[(0, e)] = lax.all_gather(stacked[-1], "col", axis=0)
    arrived = {k: along_row(far[k - 2], k) for k in range(2, rows)}

    order = [(index, e) for index in range(len(blocks)) for e in experts]
    returned = {}
    terms, home, pairs = (), [], stacked
    for position, (index, e) in enumerate(order):
        if position == 0:
            pieces = first_pieces
        elif index == 0:
            pieces = [[(gathered[(0, e)], block)] * cols for block in range(2)]
        else:
            pieces = [[(gathered[index], e * 2 + block)] * cols for block in range(2)]
        send, early, hidden, done = expand(
            e, pieces, place, norm_gain, w_gate, w_up, w_down, after=pairs
        )
        after = list(home)
        if position == 0:
            for other, ks in enumerate(blocks[1:], 1):
                layout = [[(source, e_) for e_ in experts for source in range(2)]]
                shares = stack(layout, [arrived[k] for k in ks], token=done)[0]
                gathered[other] = lax.all_gather(shares, "col", axis=0)
                after.append(shares)
        got = along_col(send, 1)
        late, *totals = contract(e, hidden, cols, place, w_down, terms=terms, after=after)
        home = []
        if totals:
            index_, e_ = order[position - 1]
            for k, total in zip(blocks[index_], totals):
                returned[k * local + e_] = along_row(total, k)
                home.append(returned[k * local + e_])
        pairs = pair_sums(early, late, got)
        terms = [along_col(share, 2 * q) for q, share in enumerate(pairs)]
    numbers = sorted(returned)
    slots = [returned[number] for number in numbers]
    partial = combine(numbers, base, ids, token_weights, tokens, slots, F32)
    index, e = order[-1]
    numbers = [k * local + e for k in blocks[index]]
    slots = [along_row(total, k) for k, total in zip(blocks[index], add(terms))]
    return combine(numbers, base, ids, token_weights, partial, slots, BF16)


def solution(mesh):
    placed = (
        P("row", "col"),
        P(),
        P("row", None),
        P("row", None),
        P("row", None, "col"),
        P("row", None, "col"),
        P("row", "col", None),
    )
    return jax.shard_map(
        functools.partial(body, mesh.shape["row"], mesh.shape["col"]),
        mesh=mesh,
        in_specs=placed,
        out_specs=P("row", "col"),
        check_vma=False,
    )
```

time: 380 us -> 218 us (0.57)
  waiting for transfers between devices: 219 us -> 42.3 us
  Pallas kernels: 0 us -> 122 us
  matrix products: 74.6 us -> 0 us
  starting transfers between devices: 4.62 us -> 36.6 us
  blocking collectives: 31.9 us -> 0 us
  other arithmetic: 19.8 us -> 0 us
  local copies, waits for them, and re-layouts: 15.8 us -> 2.04 us
    pallas_call x0 -> x19, Pallas kernels: none -> 122 us  [the longest x4 77.4 us: expand(): pl.pallas_call(functools.partial(up_kernel, expert, blocks, cols, places)...]
    reduce_scatter x1 -> x0, waiting for transfers between devices: 116 us -> none  [body(): shares = lax.psum_scatter(outputs, 'col', scatter_dimension=2, tiled=True)]
    dot_general x4 -> x0, matrix products: 74.6 us -> none  [the longest x1 25 us: run_experts(): jnp.einsum('slcf,lfd->slcd', hidden, down_block, preferred_element_type=j...]
    all_to_all x1 -> x0, waiting for transfers between devices: 47.7 us -> none  [body(): lax.all_to_all(shares, 'row', split_axis=0, concat_axis=0, tiled=True)]
    all_gather x1 -> x2, waiting for transfers between devices: 55.2 us -> 8.16 us  [the longest x1 8.16 us: body(): gathered[other] = lax.all_gather(shares, 'col', axis=0)]
    ppermute x0 -> x33, starting transfers between devices: none -> 36.6 us  [the longest x23 18.7 us: along_col(): return lax.ppermute(value, 'col', [(i, i ^ relative) for i in range(cols)])]
    ppermute x0 -> x33, waiting for transfers between devices: none -> 34.1 us  [the longest x23 19.9 us: along_col(): return lax.ppermute(value, 'col', [(i, i ^ relative) for i in range(cols)])]
    all_to_all x1 -> x0, blocking collectives: 31.9 us -> none  [body(): lax.all_to_all(packed, 'row', split_axis=0, concat_axis=0, tiled=True)]
  transfers between devices with their start and end apart: 3 -> 35, of which waited for: 3 -> 10; matrix products, arithmetic and copies ran while one was open for 0% -> 0% of each run, Pallas kernels for 0% -> 52%
where the time goes in v1:
time: 218 us; the launch traced here: 217 us
  Pallas kernels  122 us (56%)
  waiting for transfers between devices  42.3 us (19%)
  starting transfers between devices  36.6 us (17%)
  between operations  13.7 us (6%)
    pallas_call x4, Pallas kernels, expand(): pl.pallas_call(functools.partial(up_kernel, expert, blocks, cols, places)...  77.4 us
    ppermute x23, waiting for transfers between devices, along_col(): return lax.ppermute(value, 'col', [(i, i ^ relative) for i in range(cols)])  19.9 us
    pallas_call x4, Pallas kernels, contract(): pl.pallas_call(functools.partial(down_kernel, expert, count), out_shape=o...  18.7 us
    ppermute x23, starting transfers between devices, along_col(): return lax.ppermute(value, 'col', [(i, i ^ relative) for i in range(cols)])  18.7 us
    ppermute x10, starting transfers between devices, along_row(): return lax.ppermute(value, 'row', [(i, i ^ relative) for i in range(rows)])  17.8 us
    ppermute x10, waiting for transfers between devices, along_row(): return lax.ppermute(value, 'row', [(i, i ^ relative) for i in range(rows)])  14.2 us
    pallas_call x4, Pallas kernels, pair_sums(): pl.pallas_call(pair_kernel, out_shape=[jax.ShapeDtypeStruct(block, BF16)]...  9.53 us
    all_gather x1, waiting for transfers between devices, body(): gathered[other] = lax.all_gather(shares, 'col', axis=0)  8.16 us
  transfers between devices with their start and end apart: 35, of which 10 were waited for; matrix products, arithmetic and copies ran while one was open for 0% of the time, Pallas kernels for 52%

profile of v1, /device:TPU:0, one launch (start us, length us, event | category | flops | bytes accessed | tf_op | source)
XLA Modules:
  0.0 216.8 jit_solution(9512364936852497415)
XLA Ops:
  6.5 2.3 %pack.1 = (bf16[1,128,512]{2,1,0:T(8,128)(2,1)}, bf16[1,128,512]{2,1,0:T(8,128)(2,1)}, bf16[1,128,512]{2,1,0:T(8,128)(2,1)}, bf16[1,128,512]{2,1,0:T(8,128)(2,1)...) custom-call(s32[1]{0:T(128)} %bitcast.base_ref, s32[2,256]{1,0:T(2,128)} %bitcast.59, bf16[256,512]{1,0:T(8,128)(2,1)} %start_ref.1), custom_call_target="tpu_custom_call" | custom-call | tf_op jit(solution)/shard_map/pack/pallas_call | solution.py:39
  8.8 3.0 %collective-permute-start = (bf16[1,128,512]{2,1,0:T(8,128)(2,1)}, bf16[1,128,512]{2,1,0:T(8,128)(2,1)}, u32[]{:S(2)}, u32[]{:S(2)}) collective-permute-start(bf16[1,128,512]{2,1,0:T(8,128)(2,1)} %get-tuple-element.52), channel_id=1, source_target_pairs={{0,8},{8,0},{16,24},{24,16},{1,9},{9,1},{17,25},{25,17},{2,10},{10... | collective-permute-start | bytes 393224 | tf_op jit(solution)/shard_map/ppermute | solution.py:437
  11.8 3.8 %collective-permute-done.refs_1_ = bf16[1,128,512]{2,1,0:T(8,128)(2,1)} collective-permute-done((bf16[1,128,512]{2,1,0:T(8,128)(2,1)}, bf16[1,128,512]{2,1,0:T(8,128)(2,1)}, u32[]{:S(2)}, u32[]{:S(2)}) %collective-permute-start) | collective-permute-done | bytes 131104 | tf_op jit(solution)/shard_map/ppermute | solution.py:437
  15.6 1.7 stack.3.refs_19_
  17.4 1.8 collective-permute-start.1
  19.2 3.5 %collective-permute-done.1.refs_1_ = bf16[1,128,512]{2,1,0:T(8,128)(2,1)} collective-permute-done((bf16[1,128,512]{2,1,0:T(8,128)(2,1)}, bf16[1,128,512]{2,1,0:T(8,128)(2,1)}, u32[]{:S(2)}, u32[]{:S(2)}) %collective-permute-start.1) | collective-permute-done | bytes 131104 | tf_op jit(solution)/shard_map/ppermute | solution.py:437
  22.8 1.7 stack.4.refs_0_.refs_8_
  24.4 1.7 collective-permute-start.3
  26.1 1.5 collective-permute-start.5
  27.9 8.7 %collective-permute-done.3.refs_2_.refs_10_ = bf16[2,128,512]{2,1,0:T(8,128)(2,1)S(1)} collective-permute-done((bf16[2,128,512]{2,1,0:T(8,128)(2,1)}, bf16[2,128,512]{2,1,0:T(8,128)(2,1)S(1)}, u32[]{:S(2)}, u32[]{:S(2)}) %collective-permute-start.3) | collective-permute-done | bytes 262176 | tf_op jit(solution)/shard_map/ppermute | solution.py:442
  37.3 3.2 %collective-permute-done.5.refs_4_.refs_12_ = bf16[2,128,512]{2,1,0:T(8,128)(2,1)S(1)} collective-permute-done((bf16[2,128,512]{2,1,0:T(8,128)(2,1)}, bf16[2,128,512]{2,1,0:T(8,128)(2,1)S(1)}, u32[]{:S(2)}, u32[]{:S(2)}) %collective-permute-start.5) | collective-permute-done | bytes 262176 | tf_op jit(solution)/shard_map/ppermute | solution.py:442
  41.0 3.6 %collective-permute-start.10 = (bf16[2,128,512]{2,1,0:T(8,128)(2,1)}, bf16[2,128,512]{2,1,0:T(8,128)(2,1)}, u32[]{:S(2)}, u32[]{:S(2)}) collective-permute-start(bf16[2,128,512]{2,1,0:T(8,128)(2,1)} %get-tuple-element.58), channel_id=1, source_target_pairs={{0,24},{8,16},{16,8},{24,0},{1,25},{9,17},{17,9},{25,1},{2,26},{10... | collective-permute-start | bytes 786440 | tf_op jit(solution)/shard_map/ppermute | solution.py:437
  46.0 19.7 %expand.4 = (bf16[4,256,512]{2,1,0:T(8,128)(2,1)}, bf16[2,256,512]{2,1,0:T(8,128)(2,1)}, bf16[256,1792]{1,0:T(8,128)(2,1)}, s32[1]{0:T(128)}) custom-call(s32[1]{0:T(128)} %bitcast.3.place_ref, f32[8,1,512]{2,1,0:T(1,128)} %bitcast.55, bf16[2,128,512]{2,1,0:T(8,128)(2,1)} %stack.4.refs_0_.refs_8_, bf16[2,128,512]{2,1,0:T(8,128)(2,1)} %copy-done.3, ...), custom_call_target="tpu_custom_call" | custom-call | flops 10334765056 | bytes 40370176 | tf_op jit(solution)/shard_map/expand/pallas_call | solution.py:292
  65.8 1.7 collective-permute-done.9.refs_0_
  67.5 2.4 %stack.5.refs_0_ = bf16[4,128,512]{2,1,0:T(8,128)(2,1)} custom-call(bf16[2,128,512]{2,1,0:T(8,128)(2,1)} %collective-permute-done.9.refs_0_, bf16[2,128,512]{2,1,0:T(8,128)(2,1)} %collective-permute-done.10.refs_1_, s32[1]{0:T(128)} %get-tuple-element.59.refs_2_), custom_call_target="tpu_custom_call" | custom-call | tf_op jit(solution)/shard_map/stack/pallas_call | solution.py:60
  69.9 4.2 %contract.4.late_ref = bf16[2,256,512]{2,1,0:T(8,128)(2,1)} custom-call(s32[1]{0:T(128)} %bitcast.3.place_ref, bf16[256,1792]{1,0:T(8,128)(2,1)} %get-tuple-element.56.hidden_ref, bf16[2,1792,4096]{2,1,0:T(8,128)(2,1)} %w_down.7, bf16[4,128,512]{2,1,0:T(8,128)(2,1)} %stack.5.refs_0_), custom_call_target="tpu_custom_call" | custom-call | flops 60129542144 | bytes 234881024 | tf_op jit(solution)/shard_map/contract/pallas_call | solution.py:343
  74.1 2.4 %pair_sums.4 = (bf16[256,512]{1,0:T(8,128)(2,1)}, bf16[256,512]{1,0:T(8,128)(2,1)}, bf16[256,512]{1,0:T(8,128)(2,1)}, bf16[256,512]{1,0:T(8,128)(2,1)}) custom-call(bf16[2,256,512]{2,1,0:T(8,128)(2,1)} %get-tuple-element.55.early_ref, bf16[2,256,512]{2,1,0:T(8,128)(2,1)} %contract.4.late_ref, bf16[4,256,512]{2,1,0:T(8,128)(2,1)} %collective-permute-done.11.other_ref), custom_call_target="tpu_custom_call" | custom-call | tf_op jit(solution)/shard_map/pair_sums/pallas_call | solution.py:396
  76.5 1.2 collective-permute-start.12
  77.7 0.9 collective-permute-start.13
  78.6 1.5 collective-permute-start.14
  80.1 19.5 %expand.5 = (bf16[4,256,512]{2,1,0:T(8,128)(2,1)}, bf16[2,256,512]{2,1,0:T(8,128)(2,1)}, bf16[256,1792]{1,0:T(8,128)(2,1)}, s32[1]{0:T(128)}) custom-call(s32[1]{0:T(128)} %bitcast.3.place_ref, f32[8,1,512]{2,1,0:T(1,128)} %bitcast.56, bf16[8,2,128,512]{3,2,1,0:T(8,128)(2,1)} %bitcast.39, bf16[8,2,128,512]{3,2,1,0:T(8,128)(2,1)} %bitcast.40, ...), custom_call_target="tpu_custom_call" | custom-call | flops 10334765056 | bytes 40370176 | tf_op jit(solution)/shard_map/expand/pallas_call | solution.py:292
  99.7 5.3 %contract.5 = (bf16[2,256,512]{2,1,0:T(8,128)(2,1)}, bf16[128,512]{1,0:T(8,128)(2,1)}, bf16[128,512]{1,0:T(8,128)(2,1)}) custom-call(s32[1]{0:T(128)} %bitcast.3.place_ref, bf16[256,1792]{1,0:T(8,128)(2,1)} %get-tuple-element.65.hidden_ref, bf16[2,1792,4096]{2,1,0:T(8,128)(2,1)} %w_down.7, bf16[256,512]{1,0:T(8,128)(2,1)} %get-tuple-element.61.refs_19_.refs_0_, ...), custom_call_target="tpu_custom_call" | custom-call | flops 60129542144 | bytes 234881024 | tf_op jit(solution)/shard_map/contract/pallas_call | solution.py:343
  105.1 2.4 %pair_sums.5 = (bf16[256,512]{1,0:T(8,128)(2,1)}, bf16[256,512]{1,0:T(8,128)(2,1)}, bf16[256,512]{1,0:T(8,128)(2,1)}, bf16[256,512]{1,0:T(8,128)(2,1)}) custom-call(bf16[2,256,512]{2,1,0:T(8,128)(2,1)} %get-tuple-element.67.early_ref, bf16[2,256,512]{2,1,0:T(8,128)(2,1)} %get-tuple-element.68.late_ref, bf16[4,256,512]{2,1,0:T(8,128)(2,1)} %collective-permute-done.15.other_ref), custom_call_target="tpu_custom_call" | custom-call | tf_op jit(solution)/shard_map/pair_sums/pallas_call | solution.py:396
  107.5 1.2 collective-permute-start.16
  109.1 1.9 collective-permute-start.18
  111.0 8.2 %all-gather.7.cloned.1.call-done = bf16[32,128,512]{2,1,0:T(8,128)(2,1)} async-done(((bf16[4,128,512]{2,1,0:T(8,128)(2,1)}), bf16[32,128,512]{2,1,0:T(8,128)(2,1)}) %all-gather.7.cloned.1.call-update) | async-done | bytes 4194320 | tf_op jit(solution)/shard_map/all_gather | solution.py:490
  119.2 18.8 %expand.6 = (bf16[4,256,512]{2,1,0:T(8,128)(2,1)}, bf16[2,256,512]{2,1,0:T(8,128)(2,1)}, bf16[256,1792]{1,0:T(8,128)(2,1)}, s32[1]{0:T(128)}) custom-call(s32[1]{0:T(128)} %bitcast.3.place_ref, f32[8,1,512]{2,1,0:T(1,128)} %bitcast.57, bf16[8,4,128,512]{3,2,1,0:T(8,128)(2,1)} %bitcast.22, bf16[8,4,128,512]{3,2,1,0:T(8,128)(2,1)} %bitcast.8, ...), custom_call_target="tpu_custom_call" | custom-call | flops 10334765056 | bytes 40370176 | tf_op jit(solution)/shard_map/expand/pallas_call | solution.py:292
  138.3 4.6 %contract.6 = (bf16[2,256,512]{2,1,0:T(8,128)(2,1)}, bf16[128,512]{1,0:T(8,128)(2,1)}, bf16[128,512]{1,0:T(8,128)(2,1)}) custom-call(s32[1]{0:T(128)} %bitcast.3.place_ref, bf16[256,1792]{1,0:T(8,128)(2,1)} %get-tuple-element.74.hidden_ref, bf16[2,1792,4096]{2,1,0:T(8,128)(2,1)} %w_down.7, bf16[256,512]{1,0:T(8,128)(2,1)} %get-tuple-element.70.refs_19_.refs_0_, ...), custom_call_target="tpu_custom_call" | custom-call | flops 60129542144 | bytes 234881024 | tf_op jit(solution)/shard_map/contract/pallas_call | solution.py:343
  142.9 1.2 collective-permute-start.20
  144.2 2.4 %pair_sums.6 = (bf16[256,512]{1,0:T(8,128)(2,1)}, bf16[256,512]{1,0:T(8,128)(2,1)}, bf16[256,512]{1,0:T(8,128)(2,1)}, bf16[256,512]{1,0:T(8,128)(2,1)}) custom-call(bf16[2,256,512]{2,1,0:T(8,128)(2,1)} %get-tuple-element.78.early_ref, bf16[2,256,512]{2,1,0:T(8,128)(2,1)} %get-tuple-element.79.late_ref, bf16[4,256,512]{2,1,0:T(8,128)(2,1)} %collective-permute-done.21.other_ref), custom_call_target="tpu_custom_call" | custom-call | tf_op jit(solution)/shard_map/pair_sums/pallas_call | solution.py:396
  146.6 1.3 collective-permute-start.22
  147.9 1.1 collective-permute-start.23
  149.0 1.1 collective-permute-start.24
  150.1 19.5 %expand.7 = (bf16[4,256,512]{2,1,0:T(8,128)(2,1)}, bf16[2,256,512]{2,1,0:T(8,128)(2,1)}, bf16[256,1792]{1,0:T(8,128)(2,1)}, s32[1]{0:T(128)}) custom-call(s32[1]{0:T(128)} %bitcast.3.place_ref, f32[8,1,512]{2,1,0:T(1,128)} %bitcast.58, bf16[8,4,128,512]{3,2,1,0:T(8,128)(2,1)} %bitcast.23, bf16[8,4,128,512]{3,2,1,0:T(8,128)(2,1)} %bitcast.24, ...), custom_call_target="tpu_custom_call" | custom-call | flops 10334765056 | bytes 40370176 | tf_op jit(solution)/shard_map/expand/pallas_call | solution.py:292
  169.7 4.6 %contract.7 = (bf16[2,256,512]{2,1,0:T(8,128)(2,1)}, bf16[128,512]{1,0:T(8,128)(2,1)}, bf16[128,512]{1,0:T(8,128)(2,1)}) custom-call(s32[1]{0:T(128)} %bitcast.3.place_ref, bf16[256,1792]{1,0:T(8,128)(2,1)} %get-tuple-element.85.hidden_ref, bf16[2,1792,4096]{2,1,0:T(8,128)(2,1)} %w_down.7, bf16[256,512]{1,0:T(8,128)(2,1)} %get-tuple-element.81.refs_19_.refs_0_, ...), custom_call_target="tpu_custom_call" | custom-call | flops 60129542144 | bytes 234881024 | tf_op jit(solution)/shard_map/contract/pallas_call | solution.py:343
  174.3 2.4 %pair_sums.7 = (bf16[256,512]{1,0:T(8,128)(2,1)}, bf16[256,512]{1,0:T(8,128)(2,1)}, bf16[256,512]{1,0:T(8,128)(2,1)}, bf16[256,512]{1,0:T(8,128)(2,1)}) custom-call(bf16[2,256,512]{2,1,0:T(8,128)(2,1)} %get-tuple-element.88.early_ref, bf16[2,256,512]{2,1,0:T(8,128)(2,1)} %get-tuple-element.89.late_ref, bf16[4,256,512]{2,1,0:T(8,128)(2,1)} %collective-permute-done.27.other_ref), custom_call_target="tpu_custom_call" | custom-call | tf_op jit(solution)/shard_map/pair_sums/pallas_call | solution.py:396
  176.7 1.3 collective-permute-start.28
  178.1 1.2 collective-permute-start.29
  179.2 1.0 collective-permute-start.30
  180.3 4.0 %collective-permute-start.25 = (bf16[128,512]{1,0:T(8,128)(2,1)}, bf16[128,512]{1,0:T(8,128)(2,1)}, u32[]{:S(2)}, u32[]{:S(2)}) collective-permute-start(bf16[128,512]{1,0:T(8,128)(2,1)} %get-tuple-element.86), channel_id=1, source_target_pairs={{0,16},{8,24},{16,0},{24,8},{1,17},{9,25},{17,1},{25,9},{2,18},{10... | collective-permute-start | bytes 393224 | tf_op jit(solution)/shard_map/ppermute | solution.py:437
  184.3 1.9 collective-permute-done.28.refs_1_
  186.2 4.9 %collective-permute-done.29.refs_2_ = bf16[256,512]{1,0:T(8,128)(2,1)} collective-permute-done((bf16[256,512]{1,0:T(8,128)(2,1)}, bf16[256,512]{1,0:T(8,128)(2,1)}, u32[]{:S(2)}, u32[]{:S(2)}) %collective-permute-start.29) | collective-permute-done | bytes 262176 | tf_op jit(solution)/shard_map/ppermute | solution.py:442
  191.1 1.3 collective-permute-done.30.refs_3_
  192.4 2.0 add.1
  194.4 4.0 %collective-permute-start.31 = (bf16[128,512]{1,0:T(8,128)(2,1)}, bf16[128,512]{1,0:T(8,128)(2,1)}, u32[]{:S(2)}, u32[]{:S(2)}) collective-permute-start(bf16[128,512]{1,0:T(8,128)(2,1)} %get-tuple-element.95), channel_id=1, source_target_pairs={{0,16},{8,24},{16,0},{24,8},{1,17},{9,25},{17,1},{25,9},{2,18},{10... | collective-permute-start | bytes 393224 | tf_op jit(solution)/shard_map/ppermute | solution.py:437
  198.4 3.6 %combine.2.start_ref = f32[256,512]{1,0:T(8,128)} custom-call(s32[1]{0:T(128)} %bitcast.base_ref, s32[2,256]{1,0:T(2,128)} %bitcast.60, f32[2,256]{1,0:T(2,128)} %bitcast.62, bf16[256,512]{1,0:T(8,128)(2,1)} %start_ref.1, bf16[128,512]{1,0:T(8,128)(2,1)} %get-tuple-element.66.refs_4_.refs_0_, bf16[128,512]{1,0:T(8,128)(2,1)} %get-tuple-element.76.refs_4_.refs_1_, ...), custom_call_target="tpu_custom_call" | custom-call | tf_op jit(solution)/shard_map/combine/pallas_call | solution.py:97
  202.0 5.1 %collective-permute-done.31.refs_0_ = bf16[128,512]{1,0:T(8,128)(2,1)} collective-permute-done((bf16[128,512]{1,0:T(8,128)(2,1)}, bf16[128,512]{1,0:T(8,128)(2,1)}, u32[]{:S(2)}, u32[]{:S(2)}) %collective-permute-start.31) | collective-permute-done | bytes 131104 | tf_op jit(solution)/shard_map/ppermute | solution.py:437
  207.1 2.8 %combine.3 = bf16[256,512]{1,0:T(8,128)(2,1)} custom-call(s32[1]{0:T(128)} %bitcast.base_ref, s32[2,256]{1,0:T(2,128)} %bitcast.61, f32[2,256]{1,0:T(2,128)} %bitcast.63, f32[256,512]{1,0:T(8,128)} %combine.2.start_ref, bf16[128,512]{1,0:T(8,128)(2,1)} %collective-permute-done.31.refs_0_, bf16[128,512]{1,0:T(8,128)(2,1)} %collective-permute-done.32.refs_1_), custom_call_target="tpu_custom_call" | custom-call | tf_op jit(solution)/shard_map/combine/pallas_call | solution.py:97
  (57 shorter events, 4.0 us)
Async XLA Ops:
  6.5 73.5 %all-gather.5.cloned.1.call-start = ((), (), s32[]{:S(2)}) async-start(), calls=%async_computation | async-start | bytes 2359296 | tf_op jit(solution)/shard_map/all_gather | solution.py:469
  8.8 6.8 %collective-permute-start = (bf16[1,128,512]{2,1,0:T(8,128)(2,1)}, bf16[1,128,512]{2,1,0:T(8,128)(2,1)}, u32[]{:S(2)}, u32[]{:S(2)}) collective-permute-start(bf16[1,128,512]{2,1,0:T(8,128)(2,1)} %get-tuple-element.52), channel_id=1, source_target_pairs={{0,8},{8,0},{16,24},{24,16},{1,9},{9,1},{17,25},{25,17},{2,10},{10... | collective-permute-start | bytes 393224 | tf_op jit(solution)/shard_map/ppermute | solution.py:437
  17.4 101.8 %all-gather.7.cloned.1.call-start = ((), (), s32[]{:S(2)}) async-start(), calls=%async_computation.1 | async-start | bytes 4718592 | tf_op jit(solution)/shard_map/all_gather | solution.py:490
  17.4 5.3 %collective-permute-start.1 = (bf16[1,128,512]{2,1,0:T(8,128)(2,1)}, bf16[1,128,512]{2,1,0:T(8,128)(2,1)}, u32[]{:S(2)}, u32[]{:S(2)}) collective-permute-start(bf16[1,128,512]{2,1,0:T(8,128)(2,1)} %get-tuple-element.54), channel_id=1, source_target_pairs={{0,8},{8,0},{16,24},{24,16},{1,9},{9,1},{17,25},{25,17},{2,10},{10... | collective-permute-start | bytes 393224 | tf_op jit(solution)/shard_map/ppermute | solution.py:437
  24.4 12.2 %collective-permute-start.3 = (bf16[2,128,512]{2,1,0:T(8,128)(2,1)}, bf16[2,128,512]{2,1,0:T(8,128)(2,1)S(1)}, u32[]{:S(2)}, u32[]{:S(2)}) collective-permute-start(bf16[2,128,512]{2,1,0:T(8,128)(2,1)} %stack.4.refs_0_.refs_8_), channel_id=1, source_target_pairs={{0,2},{1,3},{2,0},{3,1},{4,6},{5,7},{6,4},{7,5},{8,10},{9,11},{10,... | collective-permute-start | bytes 786440 | tf_op jit(solution)/shard_map/ppermute | solution.py:442
  26.1 14.4 %collective-permute-start.5 = (bf16[2,128,512]{2,1,0:T(8,128)(2,1)}, bf16[2,128,512]{2,1,0:T(8,128)(2,1)S(1)}, u32[]{:S(2)}, u32[]{:S(2)}) collective-permute-start(bf16[2,128,512]{2,1,0:T(8,128)(2,1)} %stack.4.refs_0_.refs_8_), channel_id=1, source_target_pairs={{0,4},{1,5},{2,6},{3,7},{4,0},{5,1},{6,2},{7,3},{8,12},{9,13},{10,... | collective-permute-start | bytes 786440 | tf_op jit(solution)/shard_map/ppermute | solution.py:442
  27.6 12.9 %collective-permute-start.7 = (bf16[2,128,512]{2,1,0:T(8,128)(2,1)}, bf16[2,128,512]{2,1,0:T(8,128)(2,1)S(1)}, u32[]{:S(2)}, u32[]{:S(2)}) collective-permute-start(bf16[2,128,512]{2,1,0:T(8,128)(2,1)} %stack.4.refs_0_.refs_8_), channel_id=1, source_target_pairs={{0,6},{1,7},{2,4},{3,5},{4,2},{5,3},{6,0},{7,1},{8,14},{9,15},{10,... | collective-permute-start | bytes 786440 | tf_op jit(solution)/shard_map/ppermute | solution.py:442
  27.9 16.7 %collective-permute-start.2 = (bf16[2,128,512]{2,1,0:T(8,128)(2,1)}, bf16[2,128,512]{2,1,0:T(8,128)(2,1)S(1)}, u32[]{:S(2)}, u32[]{:S(2)}) collective-permute-start(bf16[2,128,512]{2,1,0:T(8,128)(2,1)} %stack.4.refs_0_.refs_8_), channel_id=1, source_target_pairs={{0,1},{1,0},{2,3},{3,2},{4,5},{5,4},{6,7},{7,6},{8,9},{9,8},{10,11... | collective-permute-start | bytes 786440 | tf_op jit(solution)/shard_map/ppermute | solution.py:442
  36.6 0.7 copy-start
  37.3 7.3 %collective-permute-start.4 = (bf16[2,128,512]{2,1,0:T(8,128)(2,1)S(1)}, bf16[2,128,512]{2,1,0:T(8,128)(2,1)S(1)}, u32[]{:S(2)}, u32[]{:S(2)}) collective-permute-start(bf16[2,128,512]{2,1,0:T(8,128)(2,1)S(1)} %collective-permute-done.3.refs_2_.refs_10_), channel_id=1, source_target_pairs={{0,1},{1,0},{2,3},{3,2},{4,5},{5,4},{6,7},{7,6},{8,9},{9,8},{10,11... | collective-permute-start | bytes 786440 | tf_op jit(solution)/shard_map/ppermute | solution.py:442
  40.5 4.2 %copy-start.1 = (bf16[2,128,512]{2,1,0:T(8,128)(2,1)}, bf16[2,128,512]{2,1,0:T(8,128)(2,1)S(1)}, u32[]{:S(2)}) copy-start(bf16[2,128,512]{2,1,0:T(8,128)(2,1)S(1)} %collective-permute-done.5.refs_4_.refs_12_) | copy-start | bytes 786436
  40.5 4.2 %collective-permute-start.6 = (bf16[2,128,512]{2,1,0:T(8,128)(2,1)S(1)}, bf16[2,128,512]{2,1,0:T(8,128)(2,1)S(1)}, u32[]{:S(2)}, u32[]{:S(2)}) collective-permute-start(bf16[2,128,512]{2,1,0:T(8,128)(2,1)S(1)} %collective-permute-done.5.refs_4_.refs_12_), channel_id=1, source_target_pairs={{0,1},{1,0},{2,3},{3,2},{4,5},{5,4},{6,7},{7,6},{8,9},{9,8},{10,11... | collective-permute-start | bytes 786440 | tf_op jit(solution)/shard_map/ppermute | solution.py:442
  40.5 4.2 %copy-start.2 = (bf16[2,128,512]{2,1,0:T(8,128)(2,1)}, bf16[2,128,512]{2,1,0:T(8,128)(2,1)S(1)}, u32[]{:S(2)}) copy-start(bf16[2,128,512]{2,1,0:T(8,128)(2,1)S(1)} %collective-permute-done.7.refs_6_.refs_14_) | copy-start | bytes 786436
  40.5 4.2 %collective-permute-start.8 = (bf16[2,128,512]{2,1,0:T(8,128)(2,1)S(1)}, bf16[2,128,512]{2,1,0:T(8,128)(2,1)S(1)}, u32[]{:S(2)}, u32[]{:S(2)}) collective-permute-start(bf16[2,128,512]{2,1,0:T(8,128)(2,1)S(1)} %collective-permute-done.7.refs_6_.refs_14_), channel_id=1, source_target_pairs={{0,1},{1,0},{2,3},{3,2},{4,5},{5,4},{6,7},{7,6},{8,9},{9,8},{10,11... | collective-permute-start | bytes 786440 | tf_op jit(solution)/shard_map/ppermute | solution.py:442
  41.0 24.8 %collective-permute-start.10 = (bf16[2,128,512]{2,1,0:T(8,128)(2,1)}, bf16[2,128,512]{2,1,0:T(8,128)(2,1)}, u32[]{:S(2)}, u32[]{:S(2)}) collective-permute-start(bf16[2,128,512]{2,1,0:T(8,128)(2,1)} %get-tuple-element.58), channel_id=1, source_target_pairs={{0,24},{8,16},{16,8},{24,0},{1,25},{9,17},{17,9},{25,1},{2,26},{10... | collective-permute-start | bytes 786440 | tf_op jit(solution)/shard_map/ppermute | solution.py:437
  44.6 0.7 copy-start.3
  44.6 22.9 %collective-permute-start.9 = (bf16[2,128,512]{2,1,0:T(8,128)(2,1)}, bf16[2,128,512]{2,1,0:T(8,128)(2,1)}, u32[]{:S(2)}, u32[]{:S(2)}) collective-permute-start(bf16[2,128,512]{2,1,0:T(8,128)(2,1)} %get-tuple-element.57), channel_id=1, source_target_pairs={{0,16},{8,24},{16,0},{24,8},{1,17},{9,25},{17,1},{25,9},{2,18},{10... | collective-permute-start | bytes 786440 | tf_op jit(solution)/shard_map/ppermute | solution.py:437
  44.6 0.8 copy-start.4
  44.7 0.8 copy-start.5
  45.3 0.7 copy-start.6
  65.7 8.4 %collective-permute-start.11 = (bf16[4,256,512]{2,1,0:T(8,128)(2,1)}, bf16[4,256,512]{2,1,0:T(8,128)(2,1)}, u32[]{:S(2)}, u32[]{:S(2)}) collective-permute-start(bf16[4,256,512]{2,1,0:T(8,128)(2,1)} %get-tuple-element.60), channel_id=1, source_target_pairs={{0,1},{1,0},{2,3},{3,2},{4,5},{5,4},{6,7},{7,6},{8,9},{9,8},{10,11... | collective-permute-start | bytes 3145736 | tf_op jit(solution)/shard_map/ppermute | solution.py:442
  76.5 23.1 %collective-permute-start.12 = (bf16[256,512]{1,0:T(8,128)(2,1)}, bf16[256,512]{1,0:T(8,128)(2,1)}, u32[]{:S(2)}, u32[]{:S(2)}) collective-permute-start(bf16[256,512]{1,0:T(8,128)(2,1)} %get-tuple-element.62.refs_20_), channel_id=1, source_target_pairs={{0,2},{1,3},{2,0},{3,1},{4,6},{5,7},{6,4},{7,5},{8,10},{9,11},{10,... | collective-permute-start | bytes 786440 | tf_op jit(solution)/shard_map/ppermute | solution.py:442
  77.7 22.0 %collective-permute-start.13 = (bf16[256,512]{1,0:T(8,128)(2,1)}, bf16[256,512]{1,0:T(8,128)(2,1)}, u32[]{:S(2)}, u32[]{:S(2)}) collective-permute-start(bf16[256,512]{1,0:T(8,128)(2,1)} %get-tuple-element.63.refs_21_), channel_id=1, source_target_pairs={{0,4},{1,5},{2,6},{3,7},{4,0},{5,1},{6,2},{7,3},{8,12},{9,13},{10,... | collective-permute-start | bytes 786440 | tf_op jit(solution)/shard_map/ppermute | solution.py:442
  78.6 21.1 %collective-permute-start.14 = (bf16[256,512]{1,0:T(8,128)(2,1)}, bf16[256,512]{1,0:T(8,128)(2,1)}, u32[]{:S(2)}, u32[]{:S(2)}) collective-permute-start(bf16[256,512]{1,0:T(8,128)(2,1)} %get-tuple-element.64.refs_22_), channel_id=1, source_target_pairs={{0,6},{1,7},{2,4},{3,5},{4,2},{5,3},{6,0},{7,1},{8,14},{9,15},{10,... | collective-permute-start | bytes 786440 | tf_op jit(solution)/shard_map/ppermute | solution.py:442
  99.6 5.5 %collective-permute-start.15 = (bf16[4,256,512]{2,1,0:T(8,128)(2,1)}, bf16[4,256,512]{2,1,0:T(8,128)(2,1)}, u32[]{:S(2)}, u32[]{:S(2)}) collective-permute-start(bf16[4,256,512]{2,1,0:T(8,128)(2,1)} %get-tuple-element.69), channel_id=1, source_target_pairs={{0,1},{1,0},{2,3},{3,2},{4,5},{5,4},{6,7},{7,6},{8,9},{9,8},{10,11... | collective-permute-start | bytes 3145736 | tf_op jit(solution)/shard_map/ppermute | solution.py:442
  105.0 33.3 %collective-permute-start.19 = (bf16[128,512]{1,0:T(8,128)(2,1)}, bf16[128,512]{1,0:T(8,128)(2,1)}, u32[]{:S(2)}, u32[]{:S(2)}) collective-permute-start(bf16[128,512]{1,0:T(8,128)(2,1)} %get-tuple-element.75), channel_id=1, source_target_pairs={{0,8},{8,0},{16,24},{24,16},{1,9},{9,1},{17,25},{25,17},{2,10},{10... | collective-permute-start | bytes 393224 | tf_op jit(solution)/shard_map/ppermute | solution.py:437
  107.5 30.8 %collective-permute-start.16 = (bf16[256,512]{1,0:T(8,128)(2,1)}, bf16[256,512]{1,0:T(8,128)(2,1)}, u32[]{:S(2)}, u32[]{:S(2)}) collective-permute-start(bf16[256,512]{1,0:T(8,128)(2,1)} %get-tuple-element.71.refs_20_), channel_id=1, source_target_pairs={{0,2},{1,3},{2,0},{3,1},{4,6},{5,7},{6,4},{7,5},{8,10},{9,11},{10,... | collective-permute-start | bytes 786440 | tf_op jit(solution)/shard_map/ppermute | solution.py:442
  108.7 29.6 %collective-permute-start.17 = (bf16[256,512]{1,0:T(8,128)(2,1)}, bf16[256,512]{1,0:T(8,128)(2,1)}, u32[]{:S(2)}, u32[]{:S(2)}) collective-permute-start(bf16[256,512]{1,0:T(8,128)(2,1)} %get-tuple-element.72.refs_21_), channel_id=1, source_target_pairs={{0,4},{1,5},{2,6},{3,7},{4,0},{5,1},{6,2},{7,3},{8,12},{9,13},{10,... | collective-permute-start | bytes 786440 | tf_op jit(solution)/shard_map/ppermute | solution.py:442
  109.1 29.2 %collective-permute-start.18 = (bf16[256,512]{1,0:T(8,128)(2,1)}, bf16[256,512]{1,0:T(8,128)(2,1)}, u32[]{:S(2)}, u32[]{:S(2)}) collective-permute-start(bf16[256,512]{1,0:T(8,128)(2,1)} %get-tuple-element.73.refs_22_), channel_id=1, source_target_pairs={{0,6},{1,7},{2,4},{3,5},{4,2},{5,3},{6,0},{7,1},{8,14},{9,15},{10,... | collective-permute-start | bytes 786440 | tf_op jit(solution)/shard_map/ppermute | solution.py:442
  138.0 6.2 %collective-permute-start.21 = (bf16[4,256,512]{2,1,0:T(8,128)(2,1)}, bf16[4,256,512]{2,1,0:T(8,128)(2,1)}, u32[]{:S(2)}, u32[]{:S(2)}) collective-permute-start(bf16[4,256,512]{2,1,0:T(8,128)(2,1)} %get-tuple-element.80), channel_id=1, source_target_pairs={{0,1},{1,0},{2,3},{3,2},{4,5},{5,4},{6,7},{7,6},{8,9},{9,8},{10,11... | collective-permute-start | bytes 3145736 | tf_op jit(solution)/shard_map/ppermute | solution.py:442
  142.9 26.7 %collective-permute-start.20 = (bf16[128,512]{1,0:T(8,128)(2,1)}, bf16[128,512]{1,0:T(8,128)(2,1)}, u32[]{:S(2)}, u32[]{:S(2)}) collective-permute-start(bf16[128,512]{1,0:T(8,128)(2,1)} %get-tuple-element.77), channel_id=1, source_target_pairs={{0,8},{8,0},{16,24},{24,16},{1,9},{9,1},{17,25},{25,17},{2,10},{10... | collective-permute-start | bytes 393224 | tf_op jit(solution)/shard_map/ppermute | solution.py:437
  146.6 23.1 %collective-permute-start.22 = (bf16[256,512]{1,0:T(8,128)(2,1)}, bf16[256,512]{1,0:T(8,128)(2,1)}, u32[]{:S(2)}, u32[]{:S(2)}) collective-permute-start(bf16[256,512]{1,0:T(8,128)(2,1)} %get-tuple-element.82.refs_20_), channel_id=1, source_target_pairs={{0,2},{1,3},{2,0},{3,1},{4,6},{5,7},{6,4},{7,5},{8,10},{9,11},{10,... | collective-permute-start | bytes 786440 | tf_op jit(solution)/shard_map/ppermute | solution.py:442
  147.9 21.8 %collective-permute-start.23 = (bf16[256,512]{1,0:T(8,128)(2,1)}, bf16[256,512]{1,0:T(8,128)(2,1)}, u32[]{:S(2)}, u32[]{:S(2)}) collective-permute-start(bf16[256,512]{1,0:T(8,128)(2,1)} %get-tuple-element.83.refs_21_), channel_id=1, source_target_pairs={{0,4},{1,5},{2,6},{3,7},{4,0},{5,1},{6,2},{7,3},{8,12},{9,13},{10,... | collective-permute-start | bytes 786440 | tf_op jit(solution)/shard_map/ppermute | solution.py:442
  149.0 20.7 %collective-permute-start.24 = (bf16[256,512]{1,0:T(8,128)(2,1)}, bf16[256,512]{1,0:T(8,128)(2,1)}, u32[]{:S(2)}, u32[]{:S(2)}) collective-permute-start(bf16[256,512]{1,0:T(8,128)(2,1)} %get-tuple-element.84.refs_22_), channel_id=1, source_target_pairs={{0,6},{1,7},{2,4},{3,5},{4,2},{5,3},{6,0},{7,1},{8,14},{9,15},{10,... | collective-permute-start | bytes 786440 | tf_op jit(solution)/shard_map/ppermute | solution.py:442
  169.6 4.7 %collective-permute-start.27 = (bf16[4,256,512]{2,1,0:T(8,128)(2,1)}, bf16[4,256,512]{2,1,0:T(8,128)(2,1)}, u32[]{:S(2)}, u32[]{:S(2)}) collective-permute-start(bf16[4,256,512]{2,1,0:T(8,128)(2,1)} %get-tuple-element.90), channel_id=1, source_target_pairs={{0,1},{1,0},{2,3},{3,2},{4,5},{5,4},{6,7},{7,6},{8,9},{9,8},{10,11... | collective-permute-start | bytes 3145736 | tf_op jit(solution)/shard_map/ppermute | solution.py:442
  176.7 9.5 %collective-permute-start.28 = (bf16[256,512]{1,0:T(8,128)(2,1)}, bf16[256,512]{1,0:T(8,128)(2,1)}, u32[]{:S(2)}, u32[]{:S(2)}) collective-permute-start(bf16[256,512]{1,0:T(8,128)(2,1)} %get-tuple-element.92), channel_id=1, source_target_pairs={{0,2},{1,3},{2,0},{3,1},{4,6},{5,7},{6,4},{7,5},{8,10},{9,11},{10,... | collective-permute-start | bytes 786440 | tf_op jit(solution)/shard_map/ppermute | solution.py:442
  178.1 13.0 %collective-permute-start.29 = (bf16[256,512]{1,0:T(8,128)(2,1)}, bf16[256,512]{1,0:T(8,128)(2,1)}, u32[]{:S(2)}, u32[]{:S(2)}) collective-permute-start(bf16[256,512]{1,0:T(8,128)(2,1)} %get-tuple-element.93), channel_id=1, source_target_pairs={{0,4},{1,5},{2,6},{3,7},{4,0},{5,1},{6,2},{7,3},{8,12},{9,13},{10,... | collective-permute-start | bytes 786440 | tf_op jit(solution)/shard_map/ppermute | solution.py:442
  179.2 13.1 %collective-permute-start.30 = (bf16[256,512]{1,0:T(8,128)(2,1)}, bf16[256,512]{1,0:T(8,128)(2,1)}, u32[]{:S(2)}, u32[]{:S(2)}) collective-permute-start(bf16[256,512]{1,0:T(8,128)(2,1)} %get-tuple-element.94), channel_id=1, source_target_pairs={{0,6},{1,7},{2,4},{3,5},{4,2},{5,3},{6,0},{7,1},{8,14},{9,15},{10,... | collective-permute-start | bytes 786440 | tf_op jit(solution)/shard_map/ppermute | solution.py:442
  180.3 18.1 %collective-permute-start.25 = (bf16[128,512]{1,0:T(8,128)(2,1)}, bf16[128,512]{1,0:T(8,128)(2,1)}, u32[]{:S(2)}, u32[]{:S(2)}) collective-permute-start(bf16[128,512]{1,0:T(8,128)(2,1)} %get-tuple-element.86), channel_id=1, source_target_pairs={{0,16},{8,24},{16,0},{24,8},{1,17},{9,25},{17,1},{25,9},{2,18},{10... | collective-permute-start | bytes 393224 | tf_op jit(solution)/shard_map/ppermute | solution.py:437
  184.3 14.1 %collective-permute-start.26 = (bf16[128,512]{1,0:T(8,128)(2,1)}, bf16[128,512]{1,0:T(8,128)(2,1)}, u32[]{:S(2)}, u32[]{:S(2)}) collective-permute-start(bf16[128,512]{1,0:T(8,128)(2,1)} %get-tuple-element.87), channel_id=1, source_target_pairs={{0,24},{8,16},{16,8},{24,0},{1,25},{9,17},{17,9},{25,1},{2,26},{10... | collective-permute-start | bytes 393224 | tf_op jit(solution)/shard_map/ppermute | solution.py:437
  194.4 12.7 %collective-permute-start.31 = (bf16[128,512]{1,0:T(8,128)(2,1)}, bf16[128,512]{1,0:T(8,128)(2,1)}, u32[]{:S(2)}, u32[]{:S(2)}) collective-permute-start(bf16[128,512]{1,0:T(8,128)(2,1)} %get-tuple-element.95), channel_id=1, source_target_pairs={{0,16},{8,24},{16,0},{24,8},{1,17},{9,25},{17,1},{25,9},{2,18},{10... | collective-permute-start | bytes 393224 | tf_op jit(solution)/shard_map/ppermute | solution.py:437
  198.4 8.7 %collective-permute-start.32 = (bf16[128,512]{1,0:T(8,128)(2,1)}, bf16[128,512]{1,0:T(8,128)(2,1)}, u32[]{:S(2)}, u32[]{:S(2)}) collective-permute-start(bf16[128,512]{1,0:T(8,128)(2,1)} %get-tuple-element.96), channel_id=1, source_target_pairs={{0,24},{8,16},{16,8},{24,0},{1,25},{9,17},{17,9},{25,1},{2,26},{10... | collective-permute-start | bytes 393224 | tf_op jit(solution)/shard_map/ppermute | solution.py:437
Sparse Core Ops, SparseCore 0:
  17.5 33.5 all-gather.4
  70.0 49.1 all-gather.6

commit v2 on v1

--- a/solution.py
+++ b/solution.py
@@ -8,6 +8,8 @@
 
 EXPERTS = 8
 CAP = 128
+TOK_ROW = 256
+MAIN = 320
 SLOTS = 3
 F32 = jnp.float32
 BF16 = jnp.bfloat16
@@ -47,30 +49,148 @@
 
 
 def stack_kernel(layout, count, *refs):
-    sources, out_refs = refs[:count], refs[-len(layout) :]
+    sources, index_ref, out_refs = refs[:count], refs[count], refs[-len(layout) :]
     for out_ref, parts in zip(out_refs, layout):
         for index, (source, at) in enumerate(parts):
-            out_ref[index] = sources[source][at]
-
-
-def stack(layout, sources, token=None):
+            out_ref[index] = sources[source][index_ref[at]]
+
+
+def stack(layout, sources, indices, token=None):
     tokens = () if token is None else (token,)
     vmem = pl.BlockSpec(memory_space=pltpu.VMEM)
     block = sources[0].shape[1:]
     return pl.pallas_call(
         functools.partial(stack_kernel, layout, len(sources)),
         out_shape=[jax.ShapeDtypeStruct((len(parts),) + block, BF16) for parts in layout],
-        in_specs=[vmem] * len(sources) + [pl.BlockSpec(memory_space=pltpu.SMEM)] * len(tokens),
+        in_specs=[vmem] * len(sources)
+        + [pl.BlockSpec(memory_space=pltpu.SMEM)] * (1 + len(tokens)),
         out_specs=[vmem] * len(layout),
         compiler_params=pltpu.CompilerParams(vmem_limit_bytes=VMEM),
         name="stack",
-    )(*sources, *tokens)
-
-
-def combine_kernel(experts, base_ref, ids_ref, weights_ref, start_ref, *refs):
+    )(*sources, indices, *tokens)
+
+
+def plan_kernel(rows, local, base_ref, *refs):
+    ids_refs, busy_ref, flips_ref, starts_ref, spill_ref = refs[:rows], *refs[rows:]
+    numbers = lax.broadcasted_iota(jnp.int32, (EXPERTS, TOK_ROW), 0)
+    counts = []
+    for ids_ref in ids_refs:
+        ids = jnp.bitwise_xor(ids_ref[...], base_ref[0])
+        hit = (numbers == ids[0:1, :]) | (numbers == ids[1:2, :])
+        counts.append(jnp.sum(jnp.where(hit, 1.0, 0.0), axis=1, keepdims=True))
+    loads = counts[0]
+    for count in counts[1:]:
+        loads += count
+
+    def scalar(column, expert):
+        return jnp.sum(column[expert : expert + 1, :]).astype(jnp.int32)
+
+    spill = 0
+    for k in range(rows):
+        first, second = scalar(loads, 2 * k), scalar(loads, 2 * k + 1)
+        flip = jnp.where(second > first, 1, 0)
+        flips_ref[k] = flip
+        spill = jnp.maximum(spill, jnp.minimum(first, second))
+        if k == 0:
+            small_is_first = flip
+            busy_ref[0] = flip
+            busy_ref[1] = 1 - flip
+    spill_ref[0] = spill
+    start = 0
+    for k in range(rows):
+        starts_ref[k] = start
+        first, second = scalar(counts[k], 0), scalar(counts[k], 1)
+        start = start + jnp.where(small_is_first == 1, first, second)
+    starts_ref[rows] = start
+
+
+def plan(rows, local, base, all_ids):
+    smem = pl.BlockSpec(memory_space=pltpu.SMEM)
+    vmem = pl.BlockSpec(memory_space=pltpu.VMEM)
+    sizes = [local, rows, rows + 1, 1]
+    return pl.pallas_call(
+        functools.partial(plan_kernel, rows, local),
+        out_shape=[jax.ShapeDtypeStruct((size,), jnp.int32) for size in sizes],
+        in_specs=[smem] + [vmem] * rows,
+        out_specs=[smem] * 4,
+        compiler_params=pltpu.CompilerParams(vmem_limit_bytes=VMEM),
+        name="plan",
+    )(base, *all_ids)
+
+
+def tighten_kernel(sizes, count, held, busy_ref, starts_ref, token_ref, *refs):
+    sources, out_refs = refs[:count], refs[count + held : count + held + len(sizes)]
+    begin = 0
+    for out_ref, size in zip(out_refs, sizes):
+        slot = lax.broadcasted_iota(jnp.int32, (size, CAP), 0) + begin
+        rank = lax.broadcasted_iota(jnp.int32, (size, CAP), 1)
+        total = jnp.zeros(out_ref.shape, F32)
+        for k, source in enumerate(sources):
+            at = rank + starts_ref[k]
+            picker = jnp.where((slot == at) & (at < starts_ref[k + 1]), 1.0, 0.0).astype(BF16)
+            total += jnp.dot(picker, source[busy_ref[1]], preferred_element_type=F32)
+        out_ref[...] = total.astype(BF16)
+        begin += size
+
+
+def tighten(sizes, busy, starts, token, sources, held):
+    smem = pl.BlockSpec(memory_space=pltpu.SMEM)
+    vmem = pl.BlockSpec(memory_space=pltpu.VMEM)
+    anywhere = pl.BlockSpec(memory_space=pl.ANY)
+    width, first = sources[0].shape[2], 3 + len(sources)
+    out_shape = [jax.ShapeDtypeStruct((size, width), BF16) for size in sizes]
+    out_shape += [jax.ShapeDtypeStruct(array.shape, array.dtype) for array in held]
+    return pl.pallas_call(
+        functools.partial(tighten_kernel, sizes, len(sources), len(held)),
+        out_shape=out_shape,
+        in_specs=[smem] * 3 + [vmem] * len(sources) + [anywhere] * len(held),
+        out_specs=[vmem] * len(sizes) + [anywhere] * len(held),
+        input_output_aliases={first + i: len(sizes) + i for i in range(len(held))},
+        compiler_params=pltpu.CompilerParams(vmem_limit_bytes=VMEM),
+        name="tighten",
+    )(busy, starts, token, *sources, *held)
+
+
+def loosen_kernel(rows, starts_ref, rest_ref, *refs):
+    terms, out_refs = refs[:-rows], refs[-rows:]
+    total = terms[0][...].astype(F32)
+    for term in terms[1:]:
+        total += term[...].astype(F32)
+    total = total.astype(BF16)
+    begin = 0
+    outs = [jnp.zeros(out_ref.shape, F32) for out_ref in out_refs]
+    for part in (total, rest_ref[...]):
+        slot = lax.broadcasted_iota(jnp.int32, (CAP, part.shape[0]), 1) + begin
+        rank = lax.broadcasted_iota(jnp.int32, (CAP, part.shape[0]), 0)
+        for k in range(rows):
+            at = rank + starts_ref[k]
+            picker = jnp.where((slot == at) & (at < starts_ref[k + 1]), 1.0, 0.0).astype(BF16)
+            outs[k] += jnp.dot(picker, part, preferred_element_type=F32)
+        begin += part.shape[0]
+    for out_ref, out in zip(out_refs, outs):
+        out_ref[...] = out.astype(BF16)
+
+
+def loosen(rows, starts, rest, terms):
+    vmem = pl.BlockSpec(memory_space=pltpu.VMEM)
+    block = jax.ShapeDtypeStruct((CAP, rest.shape[1]), BF16)
+    return pl.pallas_call(
+        functools.partial(loosen_kernel, rows),
+        out_shape=[block] * rows,
+        in_specs=[pl.BlockSpec(memory_space=pltpu.SMEM)] + [vmem] * (1 + len(terms)),
+        out_specs=[vmem] * rows,
+        compiler_params=pltpu.CompilerParams(vmem_limit_bytes=VMEM),
+        name="loosen",
+    )(starts, rest, *terms)
+
+
+def combine_kernel(experts, count, base_ref, flips_ref, ids_ref, weights_ref, start_ref, *refs):
     slot_refs, out_ref = refs[:-1], refs[-1]
     tokens = start_ref.shape[0]
-    ids = jnp.bitwise_xor(ids_ref[...], base_ref[0]).astype(F32)
+    ids = jnp.bitwise_xor(ids_ref[...], base_ref[0])
+    for k in range(count):
+        ids = jnp.where(ids // 2 == k, jnp.bitwise_xor(ids, flips_ref[k]), ids)
+    ids = ids.astype(F32)
     filler = jnp.zeros((4, tokens), F32)
     columns = jnp.transpose(jnp.concatenate([ids, weights_ref[...], filler], axis=0))
     lanes = lax.broadcasted_iota(jnp.int32, (tokens, 128), 1).astype(F32)
@@ -92,20 +212,22 @@
     out_ref[...] = total.astype(out_ref.dtype)
 
 
-def combine(experts, base, ids, gate_weights, start, slots, kind):
+def combine(experts, base, flips, ids, gate_weights, start, slots, kind):
+    count = flips.shape[0] if EXPERTS == 2 * flips.shape[0] else 0
     vmem = pl.BlockSpec(memory_space=pltpu.VMEM)
     return pl.pallas_call(
-        functools.partial(combine_kernel, experts),
+        functools.partial(combine_kernel, experts, count),
         out_shape=jax.ShapeDtypeStruct(start.shape, kind),
-        in_specs=[pl.BlockSpec(memory_space=pltpu.SMEM)] + [vmem] * (3 + len(slots)),
+        in_specs=[pl.BlockSpec(memory_space=pltpu.SMEM)] * 2 + [vmem] * (3 + len(slots)),
         out_specs=vmem,
         compiler_params=pltpu.CompilerParams(vmem_limit_bytes=VMEM),
         name="combine",
-    )(base, ids, gate_weights, start, *slots)
-
-
-def up_kernel(expert, blocks, cols, places, place_ref, gain_ref, *refs):
-    count = blocks * cols
+    )(base, flips, ids, gate_weights, start, *slots)
+
+
+def up_kernel(number, segments, cols, places, place_ref, experts_ref, gain_ref, *refs):
+    count = len(segments) * cols
+    expert = experts_ref[number]
     pieces = refs[:count]
     w_gate, w_up, w_down = refs[count : count + 3]
     (send_out, early_out, hidden_out, done_out, raw, scaled, ups, downs, hidden, staged, total, squares) = refs[-18:-6]
@@ -134,15 +256,17 @@
 
     def piece_copies(relative):
         copies = []
-        for block in range(blocks):
-            number = block * cols + relative
+        start = 0
+        for segment, rows in enumerate(segments):
+            number = segment * cols + relative
             piece, at = pieces[number], places[number]
-            if len(piece.shape) == 4:
-                source = piece.at[jnp.bitwise_xor(place, relative), at]
+            if at is None:
+                source = piece.at[jnp.bitwise_xor(place, relative)]
             else:
                 source = piece.at[at]
-            target = raw.at[relative, pl.ds(block * CAP, CAP), :]
+            target = raw.at[relative, pl.ds(start, rows), :]
             copies.append(pltpu.make_async_copy(source, target, x_sem.at[number]))
+            start += rows
         return copies
 
     for relative in range(cols):
@@ -153,34 +277,35 @@
     for relative in range(cols):
         for copy in piece_copies(relative):
             copy.wait()
-        if relative == 0:
-            for copy in up_copies(0):
-                copy.wait()
-            for index in range(1, slots):
-                for copy in up_copies(index):
-                    copy.start()
-        owner = jnp.bitwise_xor(place, relative)
-        at = pl.ds(pl.multiple_of(owner * width, width), width)
         values = raw[relative].astype(F32)
         square = values * values
         part = square[:, 0:128]
         for lane in range(128, width, 128):
             part += square[:, lane : lane + 128]
-        share = (values * gain_ref[owner]).astype(BF16)
+        if relative == 0:
+            squares[...] = part
+        else:
+            squares[...] += part
+    for index in range(1, slots):
+        for copy in up_copies(index):
+            copy.start()
+    mean = jnp.sum(squares[...], axis=1, keepdims=True) * (1.0 / features)
+    inverse = lax.rsqrt(mean + 1e-05)
+    for copy in up_copies(0):
+        copy.wait()
+    for relative in range(cols):
+        owner = jnp.bitwise_xor(place, relative)
+        at = pl.ds(pl.multiple_of(owner * width, width), width)
+        share = (raw[relative].astype(F32) * inverse * gain_ref[owner]).astype(BF16)
         scaled[:, at] = share
         product = jnp.dot(share, ups[0, at, :], preferred_element_type=F32)
         if relative == 0:
-            squares[...] = part
             total[...] = product
         else:
-            squares[...] += part
             total[...] += product
-    mean = jnp.sum(squares[...], axis=1, keepdims=True) * (1.0 / features)
-    squares[...] = jnp.broadcast_to(lax.rsqrt(mean + 1e-05), squares.shape)
 
     def activate(both, columns):
-        inverse = squares[:, 0:1]
-        gate, up = both[:, :tile] * inverse, both[:, tile:] * inverse
+        gate, up = both[:, :tile], both[:, tile:]
         hidden[:, columns] = (gate / (1.0 + jnp.exp(-gate)) * up).astype(BF16)
 
     activate(total[...], pl.ds(0, tile))
@@ -238,8 +363,9 @@
         out.wait()
 
 
-def down_kernel(expert, count, place_ref, hidden_ref, w_down, *refs):
+def down_kernel(number, count, place_ref, experts_ref, hidden_ref, w_down, *refs):
     terms = refs[:count]
+    expert = experts_ref[number]
     hidden, downs, staged, down_sem, out_sem, hidden_sem = refs[-6:]
     late = staged.shape[0]
 
@@ -279,10 +405,11 @@
         out.wait()
 
 
-def expand(expert, pieces, place, norm_gain, w_gate, w_up, w_down, after=()):
-    blocks, cols = len(pieces), len(pieces[0])
+def expand(number, experts, pieces, place, norm_gain, w_gate, w_up, w_down, after=()):
+    cols = len(pieces[0])
+    segments = [run[0][0].shape[-2] for run in pieces]
     features, units = w_gate.shape[1], w_gate.shape[2]
-    width, rows, half = features // cols, blocks * CAP, cols // 2
+    width, rows, half = features // cols, sum(segments), cols // 2
     tile = 256 if units % 256 == 0 else 128
     anywhere = pl.BlockSpec(memory_space=pl.ANY)
     flat = [array for block in pieces for array, _ in block]
@@ -290,7 +417,7 @@
     downs = half + half // 2
     weights = 2 * features * units + downs * units * width
     return pl.pallas_call(
-        functools.partial(up_kernel, expert, blocks, cols, places),
+        functools.partial(up_kernel, number, segments, cols, places),
         out_shape=[
             jax.ShapeDtypeStruct((half, rows, width), BF16),
             jax.ShapeDtypeStruct((half // 2, rows, width), BF16),
@@ -298,6 +425,7 @@
             jax.ShapeDtypeStruct((1,), jnp.int32),
         ],
         in_specs=[
+            pl.BlockSpec(memory_space=pltpu.SMEM),
             pl.BlockSpec(memory_space=pltpu.SMEM),
             pl.BlockSpec(memory_space=pltpu.VMEM),
         ]
@@ -324,26 +452,26 @@
             flops=2 * rows * weights, bytes_accessed=2 * weights, transcendentals=rows * units
         ),
         name="expand",
-    )(place, norm_gain.reshape(cols, 1, width), *flat, w_gate, w_up, w_down, *after)
-
-
-def contract(expert, hidden, cols, place, w_down, terms=(), after=()):
+    )(place, experts, norm_gain.reshape(cols, 1, width), *flat, w_gate, w_up, w_down, *after)
+
+
+def contract(number, experts, hidden, cols, place, w_down, terms=(), after=()):
     rows, units = hidden.shape
     width, late, count = w_down.shape[2] // cols, cols // 4, len(terms)
     anywhere = pl.BlockSpec(memory_space=pl.ANY)
     weights = units * width * late
     block = jax.ShapeDtypeStruct((CAP, width), BF16)
     side = [
-        pltpu.VMEM((count, rows, width), BF16),
-        pltpu.VMEM((rows, width), BF16),
+        pltpu.VMEM((count, 2 * CAP, width), BF16),
+        pltpu.VMEM((2 * CAP, width), BF16),
         pltpu.SemaphoreType.DMA((count,)),
         pltpu.SemaphoreType.DMA((2,)),
     ]
     out_shape = [jax.ShapeDtypeStruct((late, rows, width), BF16)] + [block, block] * bool(count)
     return pl.pallas_call(
-        functools.partial(down_kernel, expert, count),
+        functools.partial(down_kernel, number, count),
         out_shape=out_shape,
-        in_specs=[pl.BlockSpec(memory_space=pltpu.SMEM)] + [anywhere] * (2 + count + len(after)),
+        in_specs=[pl.BlockSpec(memory_space=pltpu.SMEM)] * 2 + [anywhere] * (2 + count + len(after)),
         out_specs=[anywhere] * len(out_shape),
         scratch_shapes=side * bool(count)
         + [
@@ -359,7 +487,7 @@
             flops=128 * rows * weights, bytes_accessed=128 * weights, transcendentals=0
         ),
         name="contract",
-    )(place, hidden, w_down, *terms, *after)
+    )(place, experts, hidden, w_down, *terms, *after)
 
 
 def pair_kernel(early_ref, late_ref, other_ref, *refs):
@@ -426,11 +554,7 @@
     )(*terms)
 
 
-def body(rows, cols, tokens, norm_gain, expert_ids, gate_weights, w_gate, w_up, w_down):
-    local = EXPERTS // rows
-    half = cols // 2
-    row, place = lax.axis_index("row"), lax.axis_index("col").reshape(1)
-
+def movers(rows, cols):
     def along_row(value, relative):
         if relative == 0:
             return value
@@ -448,64 +572,93 @@
         other_core = [along_col(piece, 1) for piece in same_core]
         return [piece for pair in zip(same_core, other_core) for piece in pair]
 
-    def blocks_of(pieces):
-        return [[(p, block) for p in pieces] for block in range(2)]
-
-    base = (row * local).reshape(1)
+    return along_row, along_col, gather, complete
+
+
+def blocks_of(pieces):
+    return [[(p, block) for p in pieces] for block in range(2)]
+
+
+def body_one(rows, cols, tokens, norm_gain, expert_ids, gate_weights, w_gate, w_up, w_down):
+    along_row, along_col, gather, complete = movers(rows, cols)
+    row, place = lax.axis_index("row"), lax.axis_index("col").reshape(1)
+    base = row.reshape(1)
     ids, token_weights = expert_ids.T, gate_weights.T
-    blocks = [(k, k + 1) for k in range(0, rows, 2)]
-    experts = range(local)
-    chosen = [[k * local + e] for k in range(2) for e in experts]
-    chosen += [[k * local + e for e in experts] for k in range(2, rows)]
-    packed = pack(chosen, base, ids, tokens)
-    own, sent, far = packed[:local], packed[local : 2 * local], packed[2 * local :]
-    near = [along_row(share, 1) for share in sent]
-    shares = stack([[(0, 0), (1, 0)]], [own[0], near[0]])[0]
-    first_pieces = blocks_of(complete(gather(shares)))
-    gathered = {}
-    stacked = []
-    for e in experts[1:]:
-        stacked += stack([[(0, 0), (1, 0)]], [own[e], near[e]])
-        gathered[(0, e)] = lax.all_gather(stacked[-1], "col", axis=0)
-    arrived = {k: along_row(far[k - 2], k) for k in range(2, rows)}
-
-    order = [(index, e) for index in range(len(blocks)) for e in experts]
-    returned = {}
-    terms, home, pairs = (), [], stacked
-    for position, (index, e) in enumerate(order):
-        if position == 0:
-            pieces = first_pieces
-        elif index == 0:
-            pieces = [[(gathered[(0, e)], block)] * cols for block in range(2)]
+    experts = jnp.zeros((1,), jnp.int32)
+    packed = pack([[k] for k in range(rows)], base, ids, tokens)
+    arrived = [along_row(packed[k], k) for k in range(rows)]
+    returned, pairs = [], []
+    for first in range(0, rows, 2):
+        shares = stack([[(0, 0), (1, 0)]], arrived[first : first + 2], experts)[0]
+        pieces = blocks_of(complete(gather(shares)))
+        send, early, hidden, _ = expand(
+            0, experts, pieces, place, norm_gain, w_gate, w_up, w_down, after=pairs
+        )
+        got = along_col(send, 1)
+        late = contract(0, experts, hidden, cols, place, w_down)[0]
+        pairs = pair_sums(early, late, got)
+        totals = add([along_col(share, 2 * q) for q, share in enumerate(pairs)])
+        returned += [along_row(total, first + block) for block, total in enumerate(totals)]
+    return combine(range(rows), base, base, ids, token_weights, tokens, returned, BF16)
+
+
+def body_two(rows, cols, tokens, norm_gain, expert_ids, gate_weights, w_gate, w_up, w_down):
+    along_row, along_col, gather, complete = movers(rows, cols)
+    row, place = lax.axis_index("row"), lax.axis_index("col").reshape(1)
+    base = (row * 2).reshape(1)
+    ids, token_weights = expert_ids.T, gate_weights.T
+    packed = pack([[2 * k, 2 * k + 1] for k in range(rows)], base, ids, tokens)
+    arrived = [along_row(packed[k], k) for k in range(rows)]
+    busy, flips, starts, spill = plan(rows, 2, base, [along_row(ids, k) for k in range(rows)])
+    weights = (place, norm_gain, w_gate, w_up, w_down)
+
+    def reduce(number, send, early, hidden, terms, after):
+        got = along_col(send, 1)
+        late, *totals = contract(
+            number, busy, hidden, cols, place, w_down, terms=terms, after=after
+        )
+        pairs = pair_sums(early, late, got)
+        return pairs, [along_col(share, 2 * q) for q, share in enumerate(pairs)], totals
+
+    shares = [stack([[(0, 0), (1, 0)]], arrived[k : k + 2], busy)[0] for k in range(0, rows, 2)]
+    parts = [gather(share) for share in shares]
+    pieces = blocks_of(complete(parts[0]))
+    send, early, hidden, done = expand(0, busy, pieces, *weights, after=shares[1:])
+    sizes = (MAIN, rows * CAP - MAIN)
+    main, rest, *parts[1] = tighten(sizes, busy, starts, done, arrived, parts[1])
+    everyone = lax.all_gather(main, "col", axis=0)
+    pairs, terms, _ = reduce(0, send, early, hidden, (), [main])
+    returned, home = {}, []
+    for chunk in range(1, rows // 2 + 1):
+        if chunk < rows // 2:
+            pieces, number = blocks_of(complete(parts[chunk])), 0
         else:
-            pieces = [[(gathered[index], e * 2 + block)] * cols for block in range(2)]
-        send, early, hidden, done = expand(
-            e, pieces, place, norm_gain, w_gate, w_up, w_down, after=pairs
-        )
-        after = list(home)
-        if position == 0:
-            for other, ks in enumerate(blocks[1:], 1):
-                layout = [[(source, e_) for e_ in experts for source in range(2)]]
-                shares = stack(layout, [arrived[k] for k in ks], token=done)[0]
-                gathered[other] = lax.all_gather(shares, "col", axis=0)
-                after.append(shares)
-        got = along_col(send, 1)
-        late, *totals = contract(e, hidden, cols, place, w_down, terms=terms, after=after)
+            pieces, number = [[(everyone, None)] * cols], 1
+        send, early, hidden, _ = expand(number, busy, pieces, *weights, after=pairs)
+        pairs, next_terms, totals = reduce(number, send, early, hidden, terms, home)
         home = []
-        if totals:
-            index_, e_ = order[position - 1]
-            for k, total in zip(blocks[index_], totals):
-                returned[k * local + e_] = along_row(total, k)
-                home.append(returned[k * local + e_])
-        pairs = pair_sums(early, late, got)
-        terms = [along_col(share, 2 * q) for q, share in enumerate(pairs)]
+        for k, total in zip((2 * chunk - 2, 2 * chunk - 1), totals):
+            returned[2 * k] = along_row(total, k)
+            home.append(returned[2 * k])
+        terms = next_terms
+
+    def extra(last):
+        pieces = [[(piece, 0) for piece in complete(gather(rest.reshape(1, *rest.shape)))]]
+        send, early, hidden, _ = expand(1, busy, pieces, *weights, after=[last])
+        _, terms, _ = reduce(1, send, early, hidden, (), ())
+        total = terms[0].astype(F32)
+        for term in terms[1:]:
+            total += term.astype(F32)
+        return total.astype(BF16)
+
+    more = lax.cond(spill[0] > MAIN, extra, lambda _: jnp.zeros(rest.shape, BF16), pairs[0])
     numbers = sorted(returned)
     slots = [returned[number] for number in numbers]
-    partial = combine(numbers, base, ids, token_weights, tokens, slots, F32)
-    index, e = order[-1]
-    numbers = [k * local + e for k in blocks[index]]
-    slots = [along_row(total, k) for k, total in zip(blocks[index], add(terms))]
-    return combine(numbers, base, ids, token_weights, partial, slots, BF16)
+    partial = combine(numbers, base, flips, ids, token_weights, tokens, slots, F32)
+    totals = loosen(rows, starts, more, terms)
+    slots = [along_row(total, k) for k, total in enumerate(totals)]
+    numbers = [2 * k + 1 for k in range(rows)]
+    return combine(numbers, base, flips, ids, token_weights, partial, slots, BF16)
 
 
 def solution(mesh):
@@ -518,6 +671,7 @@
         P("row", None, "col"),
         P("row", "col", None),
     )
+    body = body_two if EXPERTS == 2 * mesh.shape["row"] else body_one
     return jax.shard_map(
         functools.partial(body, mesh.shape["row"], mesh.shape["col"]),
         mesh=mesh,

time: 218 us -> 185 us (0.85)
  Pallas kernels: 122 us -> 100 us
  waiting for transfers between devices: 42.3 us -> 29.9 us
  starting transfers between devices: 36.6 us -> 39.8 us
    pallas_call x11, Pallas kernels: 105 us -> 87.1 us  [the longest x3 57.6 us: expand(): pl.pallas_call(functools.partial(up_kernel, number, segments, cols, place...]
    all_gather x2 -> x1, waiting for transfers between devices: 8.16 us -> 0.01 us  [body_two(): everyone = lax.all_gather(main, 'col', axis=0)]
    ppermute x23 -> x26, waiting for transfers between devices: 19.9 us -> 15.8 us  [along_col(): return lax.ppermute(value, 'col', [(i, i ^ relative) for i in range(cols)])]
    pallas_call x4 -> x3, Pallas kernels: 9.53 us -> 7.3 us  [pair_sums(): pl.pallas_call(pair_kernel, out_shape=[jax.ShapeDtypeStruct(block, BF16)]...]
    pallas_call x3 -> x2, Pallas kernels: 5.77 us -> 3.54 us  [stack(): pl.pallas_call(functools.partial(stack_kernel, layout, len(sources)), out...]
    ppermute x10 -> x12, starting transfers between devices: 17.8 us -> 20 us  [along_row(): return lax.ppermute(value, 'row', [(i, i ^ relative) for i in range(rows)])]
    ppermute x23 -> x26, starting transfers between devices: 18.7 us -> 19.8 us  [along_col(): return lax.ppermute(value, 'col', [(i, i ^ relative) for i in range(cols)])]
    ppermute x10 -> x12, waiting for transfers between devices: 14.2 us -> 14 us  [along_row(): return lax.ppermute(value, 'row', [(i, i ^ relative) for i in range(rows)])]
  transfers between devices with their start and end apart: 35 -> 39, of which waited for: 10 -> 7; matrix products, arithmetic and copies ran while one was open for 0% -> 0% of each run, Pallas kernels for 52% -> 48%
where the time goes in v2:
time: 185 us
  Pallas kernels  100 us (54%)
  starting transfers between devices  39.8 us (22%)
  waiting for transfers between devices  29.9 us (16%)
  between operations  14.3 us (8%)
    pallas_call x3, Pallas kernels, expand(): pl.pallas_call(functools.partial(up_kernel, number, segments, cols, place...  57.6 us
    ppermute x12, starting transfers between devices, along_row(): return lax.ppermute(value, 'row', [(i, i ^ relative) for i in range(rows)])  20 us
    ppermute x26, starting transfers between devices, along_col(): return lax.ppermute(value, 'col', [(i, i ^ relative) for i in range(cols)])  19.8 us
    ppermute x26, waiting for transfers between devices, along_col(): return lax.ppermute(value, 'col', [(i, i ^ relative) for i in range(cols)])  15.8 us
    pallas_call x3, Pallas kernels, contract(): pl.pallas_call(functools.partial(down_kernel, number, count), out_shape=o...  15.8 us
    ppermute x12, waiting for transfers between devices, along_row(): return lax.ppermute(value, 'row', [(i, i ^ relative) for i in range(rows)])  14 us
    pallas_call x3, Pallas kernels, pair_sums(): pl.pallas_call(pair_kernel, out_shape=[jax.ShapeDtypeStruct(block, BF16)]...  7.3 us
    pallas_call x2, Pallas kernels, combine(): pl.pallas_call(functools.partial(combine_kernel, experts, count), out_sha...  6.49 us
  transfers between devices with their start and end apart: 39, of which 7 were waited for; matrix products, arithmetic and copies ran while one was open for 0% of the time, Pallas kernels for 48%

profile of v2, /device:TPU:0, one launch (start us, length us, event | category | flops | bytes accessed | tf_op | source)
XLA Modules:
  0.0 184.9 jit_solution(12362724219910499813)
XLA Ops:
  6.5 2.3 %pack.1 = (bf16[2,128,512]{2,1,0:T(8,128)(2,1)}, bf16[2,128,512]{2,1,0:T(8,128)(2,1)}, bf16[2,128,512]{2,1,0:T(8,128)(2,1)}, bf16[2,128,512]{2,1,0:T(8,128)(2,1)}) custom-call(s32[1]{0:T(128)} %bitcast.2.base_ref, s32[2,256]{1,0:T(2,128)} %bitcast.26, bf16[256,512]{1,0:T(8,128)(2,1)} %start_ref.1), custom_call_target="tpu_custom_call" | custom-call | tf_op jit(solution)/shard_map/pack/pallas_call | solution.py:41
  8.9 3.0 %collective-permute-start.14 = (bf16[2,128,512]{2,1,0:T(8,128)(2,1)}, bf16[2,128,512]{2,1,0:T(8,128)(2,1)}, u32[]{:S(2)}, u32[]{:S(2)}) collective-permute-start(bf16[2,128,512]{2,1,0:T(8,128)(2,1)} %get-tuple-element.89), channel_id=1, source_target_pairs={{0,8},{8,0},{16,24},{24,16},{1,9},{9,1},{17,25},{25,17},{2,10},{10... | collective-permute-start | bytes 786440 | tf_op jit(solution)/shard_map/ppermute | solution.py:561
  11.9 3.0 %collective-permute-start.12 = (s32[2,256]{1,0:T(2,128)}, s32[2,256]{1,0:T(2,128)}, u32[]{:S(2)}, u32[]{:S(2)}) collective-permute-start(s32[2,256]{1,0:T(2,128)} %bitcast.28), channel_id=1, source_target_pairs={{0,16},{8,24},{16,0},{24,8},{1,17},{9,25},{17,1},{25,9},{2,18},{10... | collective-permute-start | bytes 6152 | tf_op jit(solution)/shard_map/ppermute | solution.py:561
  14.9 1.3 collective-permute-start.13
  16.3 1.7 collective-permute-start.22
  18.0 0.6 collective-permute-done.11.refs_1_
  18.6 3.5 %collective-permute-done.13.refs_3_ = s32[2,256]{1,0:T(2,128)} collective-permute-done((s32[2,256]{1,0:T(2,128)}, s32[2,256]{1,0:T(2,128)}, u32[]{:S(2)}, u32[]{:S(2)}) %collective-permute-start.13) | collective-permute-done | bytes 2080 | tf_op jit(solution)/shard_map/ppermute | solution.py:561
  22.1 1.4 plan.1
  23.5 1.8 stack.2.refs_0_.refs_8_
  25.3 1.5 collective-permute-start.16
  26.8 1.5 collective-permute-start.18
  28.8 1.3 collective-permute-start.23
  30.1 4.5 %collective-permute-done.22.refs_0_.refs_2_ = bf16[2,128,512]{2,1,0:T(8,128)(2,1)} collective-permute-done((bf16[2,128,512]{2,1,0:T(8,128)(2,1)}, bf16[2,128,512]{2,1,0:T(8,128)(2,1)}, u32[]{:S(2)}, u32[]{:S(2)}) %collective-permute-start.22) | collective-permute-done | bytes 262176 | tf_op jit(solution)/shard_map/ppermute | solution.py:561
  35.0 3.0 %collective-permute-done.18.refs_4_.refs_12_ = bf16[2,128,512]{2,1,0:T(8,128)(2,1)} collective-permute-done((bf16[2,128,512]{2,1,0:T(8,128)(2,1)}, bf16[2,128,512]{2,1,0:T(8,128)(2,1)}, u32[]{:S(2)}, u32[]{:S(2)}) %collective-permute-start.18) | collective-permute-done | bytes 262176 | tf_op jit(solution)/shard_map/ppermute | solution.py:566
  39.2 1.8 stack.3.refs_19_.refs_4_
  41.0 0.7 collective-permute-start.24
  41.7 1.3 collective-permute-start.25
  43.0 1.4 collective-permute-start.26
  44.5 18.5 %expand.5 = (bf16[4,256,512]{2,1,0:T(8,128)(2,1)}, bf16[2,256,512]{2,1,0:T(8,128)(2,1)}, bf16[256,1792]{1,0:T(8,128)(2,1)}, s32[1]{0:T(128)}) custom-call(s32[1]{0:T(128)} %bitcast.5.place_ref, s32[2]{0:T(128)} %get-tuple-element.86.refs_2_.experts_ref.busy_ref, f32[8,1,512]{2,1,0:T(1,128)} %bitcast.17, bf16[2,128,512]{2,1,0:T(8,128)(2,1)} %stack.2.refs_0_.refs_8_, ...), custom_call_target="tpu_custom_call" | custom-call | flops 10334765056 | bytes 40370176 | tf_op jit(solution)/shard_map/expand/pallas_call | solution.py:419
  63.0 3.1 %tighten.1 = (bf16[320,512]{1,0:T(8,128)(2,1)}, bf16[192,512]{1,0:T(8,128)(2,1)}, bf16[2,128,512]{2,1,0:T(8,128)(2,1)}, bf16[2,128,512]{2,1,0:T(8,128)(2,1)}, bf...) custom-call(s32[2]{0:T(128)} %get-tuple-element.86.refs_2_.experts_r, ...), custom_call_target="tpu_custom_call", output_to_operand_aliasing={{2}: (7, {}), {3}: (8, {}), {4}: (9, {}), {5}: (10, {})} | custom-call | tf_op jit(solution)/shard_map/tighten/pallas_call | solution.py:143
  67.2 4.9 %contract.5.late_ref = bf16[2,256,512]{2,1,0:T(8,128)(2,1)} custom-call(s32[1]{0:T(128)} %bitcast.5.place_ref, s32[2]{0:T(128)} %get-tuple-element.86.refs_2_.experts_ref.busy_ref, bf16[256,1792]{1,0:T(8,128)(2,1)} %get-tuple-element.98.hidden_ref, bf16[2,1792,4096]{2,1,0:T(8,128)(2,1)} %w_down.5, bf16[320,512]{1,0:T(8,128)(2,1)} %get-tuple-element.99.refs_0_), custom_call_target="tpu_custom_call" | custom-call | flops 60129542144 | bytes 234881024 | tf_op jit(solution)/shard_map/contract/pallas_call | solution.py:471
  72.1 2.4 %pair_sums.5 = (bf16[256,512]{1,0:T(8,128)(2,1)}, bf16[256,512]{1,0:T(8,128)(2,1)}, bf16[256,512]{1,0:T(8,128)(2,1)}, bf16[256,512]{1,0:T(8,128)(2,1)}) custom-call(bf16[2,256,512]{2,1,0:T(8,128)(2,1)} %get-tuple-element.97.early_ref, bf16[2,256,512]{2,1,0:T(8,128)(2,1)} %contract.5.late_ref, bf16[4,256,512]{2,1,0:T(8,128)(2,1)} %collective-permute-done.31.other_ref), custom_call_target="tpu_custom_call" | custom-call | tf_op jit(solution)/shard_map/pair_sums/pallas_call | solution.py:524
  74.5 0.8 collective-permute-start.32
  75.2 1.3 collective-permute-start.33
  76.6 1.4 collective-permute-start.34
  78.0 18.8 %expand.6 = (bf16[4,256,512]{2,1,0:T(8,128)(2,1)}, bf16[2,256,512]{2,1,0:T(8,128)(2,1)}, bf16[256,1792]{1,0:T(8,128)(2,1)}, s32[1]{0:T(128)}) custom-call(s32[1]{0:T(128)} %bitcast.5.place_ref, s32[2]{0:T(128)} %get-tuple-element.86.refs_2_.experts_ref.busy_ref, f32[8,1,512]{2,1,0:T(1,128)} %bitcast.18, ...), custom_call_target="tpu_custom_call" | custom-call | flops 10334765056 | bytes 40370176 | tf_op jit(solution)/shard_map/expand/pallas_call | solution.py:419
  96.9 5.3 %contract.6 = (bf16[2,256,512]{2,1,0:T(8,128)(2,1)}, bf16[128,512]{1,0:T(8,128)(2,1)}, bf16[128,512]{1,0:T(8,128)(2,1)}) custom-call(s32[1]{0:T(128)} %bitcast.5.place_ref, s32[2]{0:T(128)} %get-tuple-element.86.refs_2_.experts_ref.busy_ref, bf16[256,1792]{1,0:T(8,128)(2,1)} %get-tuple-element.105.hidden_ref, bf16[2,1792,4096]{2,1,0:T(8,128)(2,1)} %w_down.5, ...), custom_call_target="tpu_custom_call" | custom-call | flops 60129542144 | bytes 234881024 | tf_op jit(solution)/shard_map/contract/pallas_call | solution.py:471
  102.2 2.8 %collective-permute-start.35 = (bf16[128,512]{1,0:T(8,128)(2,1)}, bf16[128,512]{1,0:T(8,128)(2,1)}, u32[]{:S(2)}, u32[]{:S(2)}) collective-permute-start(bf16[128,512]{1,0:T(8,128)(2,1)} %get-tuple-element.107), channel_id=1, source_target_pairs={{0,8},{8,0},{16,24},{24,16},{1,9},{9,1},{17,25},{25,17},{2,10},{10... | collective-permute-start | bytes 393224 | tf_op jit(solution)/shard_map/ppermute | solution.py:561
  105.0 2.4 %pair_sums.6 = (bf16[256,512]{1,0:T(8,128)(2,1)}, bf16[256,512]{1,0:T(8,128)(2,1)}, bf16[256,512]{1,0:T(8,128)(2,1)}, bf16[256,512]{1,0:T(8,128)(2,1)}) custom-call(bf16[2,256,512]{2,1,0:T(8,128)(2,1)} %get-tuple-element.108.early_ref, bf16[2,256,512]{2,1,0:T(8,128)(2,1)} %get-tuple-element.109.late_ref, bf16[4,256,512]{2,1,0:T(8,128)(2,1)} %collective-permute-done.36.other_ref), custom_call_target="tpu_custom_call" | custom-call | tf_op jit(solution)/shard_map/pair_sums/pallas_call | solution.py:524
  107.4 1.5 collective-permute-start.37
  109.0 1.5 collective-permute-start.38
  111.0 20.3 %expand.7 = (bf16[4,320,512]{2,1,0:T(8,128)(2,1)}, bf16[2,320,512]{2,1,0:T(8,128)(2,1)}, bf16[320,1792]{1,0:T(8,128)(2,1)}, s32[1]{0:T(128)}) custom-call(s32[1]{0:T(128)} %bitcast.5.place_ref, s32[2]{0:T(128)} %get-tuple-element.86.refs_2_.experts_ref.busy_ref, f32[8,1,512]{2,1,0:T(1,128)} %bitcast.19, bf16[8,320,512]{2,1,0:T(8,128)(2,1)} %bitcast.9, ...), custom_call_target="tpu_custom_call" | custom-call | flops 12918456320 | bytes 40370176 | tf_op jit(solution)/shard_map/expand/pallas_call | solution.py:419
  131.4 5.6 %contract.7 = (bf16[2,320,512]{2,1,0:T(8,128)(2,1)}, bf16[128,512]{1,0:T(8,128)(2,1)}, bf16[128,512]{1,0:T(8,128)(2,1)}) custom-call(s32[1]{0:T(128)} %bitcast.5.place_ref, s32[2]{0:T(128)} %get-tuple-element.86.refs_2_.experts_ref.busy_ref, bf16[320,1792]{1,0:T(8,128)(2,1)} %get-tuple-element.115.hidden_ref, bf16[2,1792,4096]{2,1,0:T(8,128)(2,1)} %w_down.5, ...), custom_call_target="tpu_custom_call" | custom-call | flops 75161927680 | bytes 234881024 | tf_op jit(solution)/shard_map/contract/pallas_call | solution.py:471
  137.0 2.6 %pair_sums.7 = (bf16[320,512]{1,0:T(8,128)(2,1)}, bf16[320,512]{1,0:T(8,128)(2,1)}, bf16[320,512]{1,0:T(8,128)(2,1)}, bf16[320,512]{1,0:T(8,128)(2,1)}) custom-call(bf16[2,320,512]{2,1,0:T(8,128)(2,1)} %get-tuple-element.120.early_ref, bf16[2,320,512]{2,1,0:T(8,128)(2,1)} %get-tuple-element.121.late_ref, bf16[4,320,512]{2,1,0:T(8,128)(2,1)} %collective-permute-done.42.other_ref), custom_call_target="tpu_custom_call" | custom-call | tf_op jit(solution)/shard_map/pair_sums/pallas_call | solution.py:524
  139.6 1.5 collective-permute-start.43
  141.2 0.7 conditional.1
  141.2 0.7 broadcast.2
  141.9 1.5 collective-permute-start.44
  143.9 1.0 collective-permute-start.40
  144.8 1.4 collective-permute-start.41
  146.3 4.2 %collective-permute-done.43.refs_1_ = bf16[320,512]{1,0:T(8,128)(2,1)} collective-permute-done((bf16[320,512]{1,0:T(8,128)(2,1)}, bf16[320,512]{1,0:T(8,128)(2,1)}, u32[]{:S(2)}, u32[]{:S(2)}) %collective-permute-start.43) | collective-permute-done | bytes 327712 | tf_op jit(solution)/shard_map/ppermute | solution.py:566
  150.5 8.5 %collective-permute-done.44.refs_2_ = bf16[320,512]{1,0:T(8,128)(2,1)} collective-permute-done((bf16[320,512]{1,0:T(8,128)(2,1)}, bf16[320,512]{1,0:T(8,128)(2,1)}, u32[]{:S(2)}, u32[]{:S(2)}) %collective-permute-start.44) | collective-permute-done | bytes 327712 | tf_op jit(solution)/shard_map/ppermute | solution.py:566
  159.0 2.7 %loosen.1 = (bf16[128,512]{1,0:T(8,128)(2,1)}, bf16[128,512]{1,0:T(8,128)(2,1)}, bf16[128,512]{1,0:T(8,128)(2,1)}, bf16[128,512]{1,0:T(8,128)(2,1)}) custom-call(s32[5]{0:T(128)} %get-tuple-element.87.starts_ref, bf16[192,512]{1,0:T(8,128)(2,1)} %get-tuple-element.131.rest_ref, bf16[320,512]{1,0:T(8,128)(2,1)} %get-tuple-element.123.refs_0_, ...), custom_call_target="tpu_custom_call" | custom-call | tf_op jit(solution)/shard_map/loosen/pallas_call | solution.py:177
  161.7 3.0 %collective-permute-start.47 = (bf16[128,512]{1,0:T(8,128)(2,1)}, bf16[128,512]{1,0:T(8,128)(2,1)}, u32[]{:S(2)}, u32[]{:S(2)}) collective-permute-start(bf16[128,512]{1,0:T(8,128)(2,1)} %get-tuple-element.129), channel_id=1, source_target_pairs={{0,16},{8,24},{16,0},{24,8},{1,17},{9,25},{17,1},{25,9},{2,18},{10... | collective-permute-start | bytes 393224 | tf_op jit(solution)/shard_map/ppermute | solution.py:561
  164.7 1.4 collective-permute-start.48
  166.1 3.3 %combine.2.start_ref = f32[256,512]{1,0:T(8,128)} custom-call(s32[1]{0:T(128)} %bitcast.2.base_ref, s32[4]{0:T(128)} %get-tuple-element.85.flips_ref, s32[2,256]{1,0:T(2,128)} %bitcast.31, f32[2,256]{1,0:T(2,128)} %bitcast.33, bf16[256,512]{1,0:T(8,128)(2,1)} %start_ref.1, bf16[128,512]{1,0:T(8,128)(2,1)} %get-tuple-element.106.refs_4_.refs_0_, ...), custom_call_target="tpu_custom_call" | custom-call | tf_op jit(solution)/shard_map/combine/pallas_call | solution.py:218
  169.3 5.4 %collective-permute-done.47.refs_2_ = bf16[128,512]{1,0:T(8,128)(2,1)} collective-permute-done((bf16[128,512]{1,0:T(8,128)(2,1)}, bf16[128,512]{1,0:T(8,128)(2,1)}, u32[]{:S(2)}, u32[]{:S(2)}) %collective-permute-start.47) | collective-permute-done | bytes 131104 | tf_op jit(solution)/shard_map/ppermute | solution.py:561
  174.8 3.2 %combine.3 = bf16[256,512]{1,0:T(8,128)(2,1)} custom-call(s32[1]{0:T(128)} %bitcast.2.base_ref, s32[4]{0:T(128)} %get-tuple-element.85.flips_ref, s32[2,256]{1,0:T(2,128)} %bitcast.32, f32[2,256]{1,0:T(2,128)} %bitcast.34, f32[256,512]{1,0:T(8,128)} %combine.2.start_ref, bf16[128,512]{1,0:T(8,128)(2,1)} %get-tuple-element.127.refs_0_, ...), custom_call_target="tpu_custom_call" | custom-call | tf_op jit(solution)/shard_map/combine/pallas_call | solution.py:218
  (50 shorter events, 3.7 us)
Async XLA Ops:
  6.5 104.4 %all-gather.3.cloned.1.call-start = ((), (), s32[]{:S(2)}) async-start(), calls=%async_computation | async-start | bytes 2949120 | tf_op jit(solution)/shard_map/all_gather | solution.py:629
  8.9 14.6 %collective-permute-start.14 = (bf16[2,128,512]{2,1,0:T(8,128)(2,1)}, bf16[2,128,512]{2,1,0:T(8,128)(2,1)}, u32[]{:S(2)}, u32[]{:S(2)}) collective-permute-start(bf16[2,128,512]{2,1,0:T(8,128)(2,1)} %get-tuple-element.89), channel_id=1, source_target_pairs={{0,8},{8,0},{16,24},{24,16},{1,9},{9,1},{17,25},{25,17},{2,10},{10... | collective-permute-start | bytes 786440 | tf_op jit(solution)/shard_map/ppermute | solution.py:561
  11.9 6.7 %collective-permute-start.11 = (s32[2,256]{1,0:T(2,128)}, s32[2,256]{1,0:T(2,128)}, u32[]{:S(2)}, u32[]{:S(2)}) collective-permute-start(s32[2,256]{1,0:T(2,128)} %bitcast.27), channel_id=1, source_target_pairs={{0,8},{8,0},{16,24},{24,16},{1,9},{9,1},{17,25},{25,17},{2,10},{10... | collective-permute-start | bytes 6152 | tf_op jit(solution)/shard_map/ppermute | solution.py:561
  11.9 6.7 %collective-permute-start.12 = (s32[2,256]{1,0:T(2,128)}, s32[2,256]{1,0:T(2,128)}, u32[]{:S(2)}, u32[]{:S(2)}) collective-permute-start(s32[2,256]{1,0:T(2,128)} %bitcast.28), channel_id=1, source_target_pairs={{0,16},{8,24},{16,0},{24,8},{1,17},{9,25},{17,1},{25,9},{2,18},{10... | collective-permute-start | bytes 6152 | tf_op jit(solution)/shard_map/ppermute | solution.py:561
  14.9 7.2 %collective-permute-start.13 = (s32[2,256]{1,0:T(2,128)}, s32[2,256]{1,0:T(2,128)}, u32[]{:S(2)}, u32[]{:S(2)}) collective-permute-start(s32[2,256]{1,0:T(2,128)} %bitcast.29), channel_id=1, source_target_pairs={{0,24},{8,16},{16,8},{24,0},{1,25},{9,17},{17,9},{25,1},{2,26},{10... | collective-permute-start | bytes 6152 | tf_op jit(solution)/shard_map/ppermute | solution.py:561
  16.3 18.3 %collective-permute-start.22 = (bf16[2,128,512]{2,1,0:T(8,128)(2,1)}, bf16[2,128,512]{2,1,0:T(8,128)(2,1)}, u32[]{:S(2)}, u32[]{:S(2)}) collective-permute-start(bf16[2,128,512]{2,1,0:T(8,128)(2,1)} %get-tuple-element.90), channel_id=1, source_target_pairs={{0,16},{8,24},{16,0},{24,8},{1,17},{9,25},{17,1},{25,9},{2,18},{10... | collective-permute-start | bytes 786440 | tf_op jit(solution)/shard_map/ppermute | solution.py:561
  25.3 9.3 %collective-permute-start.16 = (bf16[2,128,512]{2,1,0:T(8,128)(2,1)}, bf16[2,128,512]{2,1,0:T(8,128)(2,1)}, u32[]{:S(2)}, u32[]{:S(2)}) collective-permute-start(bf16[2,128,512]{2,1,0:T(8,128)(2,1)} %stack.2.refs_0_.refs_8_), channel_id=1, source_target_pairs={{0,2},{1,3},{2,0},{3,1},{4,6},{5,7},{6,4},{7,5},{8,10},{9,11},{10,... | collective-permute-start | bytes 786440 | tf_op jit(solution)/shard_map/ppermute | solution.py:566
  26.8 11.3 %collective-permute-start.18 = (bf16[2,128,512]{2,1,0:T(8,128)(2,1)}, bf16[2,128,512]{2,1,0:T(8,128)(2,1)}, u32[]{:S(2)}, u32[]{:S(2)}) collective-permute-start(bf16[2,128,512]{2,1,0:T(8,128)(2,1)} %stack.2.refs_0_.refs_8_), channel_id=1, source_target_pairs={{0,4},{1,5},{2,6},{3,7},{4,0},{5,1},{6,2},{7,3},{8,12},{9,13},{10,... | collective-permute-start | bytes 786440 | tf_op jit(solution)/shard_map/ppermute | solution.py:566
  28.3 9.8 %collective-permute-start.20 = (bf16[2,128,512]{2,1,0:T(8,128)(2,1)}, bf16[2,128,512]{2,1,0:T(8,128)(2,1)}, u32[]{:S(2)}, u32[]{:S(2)}) collective-permute-start(bf16[2,128,512]{2,1,0:T(8,128)(2,1)} %stack.2.refs_0_.refs_8_), channel_id=1, source_target_pairs={{0,6},{1,7},{2,4},{3,5},{4,2},{5,3},{6,0},{7,1},{8,14},{9,15},{10,... | collective-permute-start | bytes 786440 | tf_op jit(solution)/shard_map/ppermute | solution.py:566
  28.8 10.4 %collective-permute-start.23 = (bf16[2,128,512]{2,1,0:T(8,128)(2,1)}, bf16[2,128,512]{2,1,0:T(8,128)(2,1)}, u32[]{:S(2)}, u32[]{:S(2)}) collective-permute-start(bf16[2,128,512]{2,1,0:T(8,128)(2,1)} %get-tuple-element.91), channel_id=1, source_target_pairs={{0,24},{8,16},{16,8},{24,0},{1,25},{9,17},{17,9},{25,1},{2,26},{10... | collective-permute-start | bytes 786440 | tf_op jit(solution)/shard_map/ppermute | solution.py:561
  34.5 7.2 %collective-permute-start.15 = (bf16[2,128,512]{2,1,0:T(8,128)(2,1)}, bf16[2,128,512]{2,1,0:T(8,128)(2,1)}, u32[]{:S(2)}, u32[]{:S(2)}) collective-permute-start(bf16[2,128,512]{2,1,0:T(8,128)(2,1)} %stack.2.refs_0_.refs_8_), channel_id=1, source_target_pairs={{0,1},{1,0},{2,3},{3,2},{4,5},{5,4},{6,7},{7,6},{8,9},{9,8},{10,11... | collective-permute-start | bytes 786440 | tf_op jit(solution)/shard_map/ppermute | solution.py:566
  34.5 8.5 %collective-permute-start.17 = (bf16[2,128,512]{2,1,0:T(8,128)(2,1)}, bf16[2,128,512]{2,1,0:T(8,128)(2,1)}, u32[]{:S(2)}, u32[]{:S(2)}) collective-permute-start(bf16[2,128,512]{2,1,0:T(8,128)(2,1)} %collective-permute-done.16.refs_2_.refs_10_), channel_id=1, source_target_pairs={{0,1},{1,0},{2,3},{3,2},{4,5},{5,4},{6,7},{7,6},{8,9},{9,8},{10,11... | collective-permute-start | bytes 786440 | tf_op jit(solution)/shard_map/ppermute | solution.py:566
  38.0 6.4 %collective-permute-start.19 = (bf16[2,128,512]{2,1,0:T(8,128)(2,1)}, bf16[2,128,512]{2,1,0:T(8,128)(2,1)}, u32[]{:S(2)}, u32[]{:S(2)}) collective-permute-start(bf16[2,128,512]{2,1,0:T(8,128)(2,1)} %collective-permute-done.18.refs_4_.refs_12_), channel_id=1, source_target_pairs={{0,1},{1,0},{2,3},{3,2},{4,5},{5,4},{6,7},{7,6},{8,9},{9,8},{10,11... | collective-permute-start | bytes 786440 | tf_op jit(solution)/shard_map/ppermute | solution.py:566
  38.1 6.4 %collective-permute-start.21 = (bf16[2,128,512]{2,1,0:T(8,128)(2,1)}, bf16[2,128,512]{2,1,0:T(8,128)(2,1)}, u32[]{:S(2)}, u32[]{:S(2)}) collective-permute-start(bf16[2,128,512]{2,1,0:T(8,128)(2,1)} %collective-permute-done.20.refs_6_.refs_14_), channel_id=1, source_target_pairs={{0,1},{1,0},{2,3},{3,2},{4,5},{5,4},{6,7},{7,6},{8,9},{9,8},{10,11... | collective-permute-start | bytes 786440 | tf_op jit(solution)/shard_map/ppermute | solution.py:566
  41.0 22.0 %collective-permute-start.24 = (bf16[2,128,512]{2,1,0:T(8,128)(2,1)}, bf16[2,128,512]{2,1,0:T(8,128)(2,1)}, u32[]{:S(2)}, u32[]{:S(2)}) collective-permute-start(bf16[2,128,512]{2,1,0:T(8,128)(2,1)} %stack.3.refs_19_.refs_4_), channel_id=1, source_target_pairs={{0,2},{1,3},{2,0},{3,1},{4,6},{5,7},{6,4},{7,5},{8,10},{9,11},{10,... | collective-permute-start | bytes 786440 | tf_op jit(solution)/shard_map/ppermute | solution.py:566
  41.7 21.3 %collective-permute-start.25 = (bf16[2,128,512]{2,1,0:T(8,128)(2,1)}, bf16[2,128,512]{2,1,0:T(8,128)(2,1)}, u32[]{:S(2)}, u32[]{:S(2)}) collective-permute-start(bf16[2,128,512]{2,1,0:T(8,128)(2,1)} %stack.3.refs_19_.refs_4_), channel_id=1, source_target_pairs={{0,4},{1,5},{2,6},{3,7},{4,0},{5,1},{6,2},{7,3},{8,12},{9,13},{10,... | collective-permute-start | bytes 786440 | tf_op jit(solution)/shard_map/ppermute | solution.py:566
  43.0 20.0 %collective-permute-start.26 = (bf16[2,128,512]{2,1,0:T(8,128)(2,1)}, bf16[2,128,512]{2,1,0:T(8,128)(2,1)}, u32[]{:S(2)}, u32[]{:S(2)}) collective-permute-start(bf16[2,128,512]{2,1,0:T(8,128)(2,1)} %stack.3.refs_19_.refs_4_), channel_id=1, source_target_pairs={{0,6},{1,7},{2,4},{3,5},{4,2},{5,3},{6,0},{7,1},{8,14},{9,15},{10,... | collective-permute-start | bytes 786440 | tf_op jit(solution)/shard_map/ppermute | solution.py:566
  66.2 9.1 %collective-permute-start.27 = (bf16[2,128,512]{2,1,0:T(8,128)(2,1)}, bf16[2,128,512]{2,1,0:T(8,128)(2,1)}, u32[]{:S(2)}, u32[]{:S(2)}) collective-permute-start(bf16[2,128,512]{2,1,0:T(8,128)(2,1)} %get-tuple-element.93.refs_0_.refs_8_), channel_id=1, source_target_pairs={{0,1},{1,0},{2,3},{3,2},{4,5},{5,4},{6,7},{7,6},{8,9},{9,8},{10,11... | collective-permute-start | bytes 786440 | tf_op jit(solution)/shard_map/ppermute | solution.py:566
  66.2 10.4 %collective-permute-start.28 = (bf16[2,128,512]{2,1,0:T(8,128)(2,1)}, bf16[2,128,512]{2,1,0:T(8,128)(2,1)}, u32[]{:S(2)}, u32[]{:S(2)}) collective-permute-start(bf16[2,128,512]{2,1,0:T(8,128)(2,1)} %get-tuple-element.94.refs_2_.refs_10_), channel_id=1, source_target_pairs={{0,1},{1,0},{2,3},{3,2},{4,5},{5,4},{6,7},{7,6},{8,9},{9,8},{10,11... | collective-permute-start | bytes 786440 | tf_op jit(solution)/shard_map/ppermute | solution.py:566
  66.7 11.4 %collective-permute-start.29 = (bf16[2,128,512]{2,1,0:T(8,128)(2,1)}, bf16[2,128,512]{2,1,0:T(8,128)(2,1)}, u32[]{:S(2)}, u32[]{:S(2)}) collective-permute-start(bf16[2,128,512]{2,1,0:T(8,128)(2,1)} %get-tuple-element.95.refs_4_.refs_12_), channel_id=1, source_target_pairs={{0,1},{1,0},{2,3},{3,2},{4,5},{5,4},{6,7},{7,6},{8,9},{9,8},{10,11... | collective-permute-start | bytes 786440 | tf_op jit(solution)/shard_map/ppermute | solution.py:566
  66.7 11.4 %collective-permute-start.30 = (bf16[2,128,512]{2,1,0:T(8,128)(2,1)}, bf16[2,128,512]{2,1,0:T(8,128)(2,1)}, u32[]{:S(2)}, u32[]{:S(2)}) collective-permute-start(bf16[2,128,512]{2,1,0:T(8,128)(2,1)} %get-tuple-element.96.refs_6_.refs_14_), channel_id=1, source_target_pairs={{0,1},{1,0},{2,3},{3,2},{4,5},{5,4},{6,7},{7,6},{8,9},{9,8},{10,11... | collective-permute-start | bytes 786440 | tf_op jit(solution)/shard_map/ppermute | solution.py:566
  67.2 4.9 %collective-permute-start.31 = (bf16[4,256,512]{2,1,0:T(8,128)(2,1)}, bf16[4,256,512]{2,1,0:T(8,128)(2,1)}, u32[]{:S(2)}, u32[]{:S(2)}) collective-permute-start(bf16[4,256,512]{2,1,0:T(8,128)(2,1)} %get-tuple-element.100), channel_id=1, source_target_pairs={{0,1},{1,0},{2,3},{3,2},{4,5},{5,4},{6,7},{7,6},{8,9},{9,8},{10,11... | collective-permute-start | bytes 3145736 | tf_op jit(solution)/shard_map/ppermute | solution.py:566
  74.5 22.4 %collective-permute-start.32 = (bf16[256,512]{1,0:T(8,128)(2,1)}, bf16[256,512]{1,0:T(8,128)(2,1)}, u32[]{:S(2)}, u32[]{:S(2)}) collective-permute-start(bf16[256,512]{1,0:T(8,128)(2,1)} %get-tuple-element.102.refs_20_), channel_id=1, source_target_pairs={{0,2},{1,3},{2,0},{3,1},{4,6},{5,7},{6,4},{7,5},{8,10},{9,11},{10,... | collective-permute-start | bytes 786440 | tf_op jit(solution)/shard_map/ppermute | solution.py:566
  75.2 21.7 %collective-permute-start.33 = (bf16[256,512]{1,0:T(8,128)(2,1)}, bf16[256,512]{1,0:T(8,128)(2,1)}, u32[]{:S(2)}, u32[]{:S(2)}) collective-permute-start(bf16[256,512]{1,0:T(8,128)(2,1)} %get-tuple-element.103.refs_21_), channel_id=1, source_target_pairs={{0,4},{1,5},{2,6},{3,7},{4,0},{5,1},{6,2},{7,3},{8,12},{9,13},{10,... | collective-permute-start | bytes 786440 | tf_op jit(solution)/shard_map/ppermute | solution.py:566
  76.6 20.3 %collective-permute-start.34 = (bf16[256,512]{1,0:T(8,128)(2,1)}, bf16[256,512]{1,0:T(8,128)(2,1)}, u32[]{:S(2)}, u32[]{:S(2)}) collective-permute-start(bf16[256,512]{1,0:T(8,128)(2,1)} %get-tuple-element.104.refs_22_), channel_id=1, source_target_pairs={{0,6},{1,7},{2,4},{3,5},{4,2},{5,3},{6,0},{7,1},{8,14},{9,15},{10,... | collective-permute-start | bytes 786440 | tf_op jit(solution)/shard_map/ppermute | solution.py:566
  96.8 8.2 %collective-permute-start.36 = (bf16[4,256,512]{2,1,0:T(8,128)(2,1)}, bf16[4,256,512]{2,1,0:T(8,128)(2,1)}, u32[]{:S(2)}, u32[]{:S(2)}) collective-permute-start(bf16[4,256,512]{2,1,0:T(8,128)(2,1)} %get-tuple-element.110), channel_id=1, source_target_pairs={{0,1},{1,0},{2,3},{3,2},{4,5},{5,4},{6,7},{7,6},{8,9},{9,8},{10,11... | collective-permute-start | bytes 3145736 | tf_op jit(solution)/shard_map/ppermute | solution.py:566
  102.2 29.1 %collective-permute-start.35 = (bf16[128,512]{1,0:T(8,128)(2,1)}, bf16[128,512]{1,0:T(8,128)(2,1)}, u32[]{:S(2)}, u32[]{:S(2)}) collective-permute-start(bf16[128,512]{1,0:T(8,128)(2,1)} %get-tuple-element.107), channel_id=1, source_target_pairs={{0,8},{8,0},{16,24},{24,16},{1,9},{9,1},{17,25},{25,17},{2,10},{10... | collective-permute-start | bytes 393224 | tf_op jit(solution)/shard_map/ppermute | solution.py:561
  107.4 24.0 %collective-permute-start.37 = (bf16[256,512]{1,0:T(8,128)(2,1)}, bf16[256,512]{1,0:T(8,128)(2,1)}, u32[]{:S(2)}, u32[]{:S(2)}) collective-permute-start(bf16[256,512]{1,0:T(8,128)(2,1)} %get-tuple-element.112.refs_12_), channel_id=1, source_target_pairs={{0,2},{1,3},{2,0},{3,1},{4,6},{5,7},{6,4},{7,5},{8,10},{9,11},{10,... | collective-permute-start | bytes 786440 | tf_op jit(solution)/shard_map/ppermute | solution.py:566
  109.0 22.4 %collective-permute-start.38 = (bf16[256,512]{1,0:T(8,128)(2,1)}, bf16[256,512]{1,0:T(8,128)(2,1)}, u32[]{:S(2)}, u32[]{:S(2)}) collective-permute-start(bf16[256,512]{1,0:T(8,128)(2,1)} %get-tuple-element.113.refs_13_), channel_id=1, source_target_pairs={{0,4},{1,5},{2,6},{3,7},{4,0},{5,1},{6,2},{7,3},{8,12},{9,13},{10,... | collective-permute-start | bytes 786440 | tf_op jit(solution)/shard_map/ppermute | solution.py:566
  110.5 20.9 %collective-permute-start.39 = (bf16[256,512]{1,0:T(8,128)(2,1)}, bf16[256,512]{1,0:T(8,128)(2,1)}, u32[]{:S(2)}, u32[]{:S(2)}) collective-permute-start(bf16[256,512]{1,0:T(8,128)(2,1)} %get-tuple-element.114.refs_14_), channel_id=1, source_target_pairs={{0,6},{1,7},{2,4},{3,5},{4,2},{5,3},{6,0},{7,1},{8,14},{9,15},{10,... | collective-permute-start | bytes 786440 | tf_op jit(solution)/shard_map/ppermute | solution.py:566
  131.3 5.7 %collective-permute-start.42 = (bf16[4,320,512]{2,1,0:T(8,128)(2,1)}, bf16[4,320,512]{2,1,0:T(8,128)(2,1)}, u32[]{:S(2)}, u32[]{:S(2)}) collective-permute-start(bf16[4,320,512]{2,1,0:T(8,128)(2,1)} %get-tuple-element.122), channel_id=1, source_target_pairs={{0,1},{1,0},{2,3},{3,2},{4,5},{5,4},{6,7},{7,6},{8,9},{9,8},{10,11... | collective-permute-start | bytes 3932168 | tf_op jit(solution)/shard_map/ppermute | solution.py:566
  139.6 10.9 %collective-permute-start.43 = (bf16[320,512]{1,0:T(8,128)(2,1)}, bf16[320,512]{1,0:T(8,128)(2,1)}, u32[]{:S(2)}, u32[]{:S(2)}) collective-permute-start(bf16[320,512]{1,0:T(8,128)(2,1)} %get-tuple-element.124), channel_id=1, source_target_pairs={{0,2},{1,3},{2,0},{3,1},{4,6},{5,7},{6,4},{7,5},{8,10},{9,11},{10,... | collective-permute-start | bytes 983048 | tf_op jit(solution)/shard_map/ppermute | solution.py:566
  141.9 17.1 %collective-permute-start.44 = (bf16[320,512]{1,0:T(8,128)(2,1)}, bf16[320,512]{1,0:T(8,128)(2,1)}, u32[]{:S(2)}, u32[]{:S(2)}) collective-permute-start(bf16[320,512]{1,0:T(8,128)(2,1)} %get-tuple-element.125), channel_id=1, source_target_pairs={{0,4},{1,5},{2,6},{3,7},{4,0},{5,1},{6,2},{7,3},{8,12},{9,13},{10,... | collective-permute-start | bytes 983048 | tf_op jit(solution)/shard_map/ppermute | solution.py:566
  143.4 15.6 %collective-permute-start.45 = (bf16[320,512]{1,0:T(8,128)(2,1)}, bf16[320,512]{1,0:T(8,128)(2,1)}, u32[]{:S(2)}, u32[]{:S(2)}) collective-permute-start(bf16[320,512]{1,0:T(8,128)(2,1)} %get-tuple-element.126), channel_id=1, source_target_pairs={{0,6},{1,7},{2,4},{3,5},{4,2},{5,3},{6,0},{7,1},{8,14},{9,15},{10,... | collective-permute-start | bytes 983048 | tf_op jit(solution)/shard_map/ppermute | solution.py:566
  143.9 22.2 %collective-permute-start.40 = (bf16[128,512]{1,0:T(8,128)(2,1)}, bf16[128,512]{1,0:T(8,128)(2,1)}, u32[]{:S(2)}, u32[]{:S(2)}) collective-permute-start(bf16[128,512]{1,0:T(8,128)(2,1)} %get-tuple-element.116), channel_id=1, source_target_pairs={{0,16},{8,24},{16,0},{24,8},{1,17},{9,25},{17,1},{25,9},{2,18},{10... | collective-permute-start | bytes 393224 | tf_op jit(solution)/shard_map/ppermute | solution.py:561
  144.8 21.3 %collective-permute-start.41 = (bf16[128,512]{1,0:T(8,128)(2,1)}, bf16[128,512]{1,0:T(8,128)(2,1)}, u32[]{:S(2)}, u32[]{:S(2)}) collective-permute-start(bf16[128,512]{1,0:T(8,128)(2,1)} %get-tuple-element.117), channel_id=1, source_target_pairs={{0,24},{8,16},{16,8},{24,0},{1,25},{9,17},{17,9},{25,1},{2,26},{10... | collective-permute-start | bytes 393224 | tf_op jit(solution)/shard_map/ppermute | solution.py:561
  161.7 7.7 %collective-permute-start.46 = (bf16[128,512]{1,0:T(8,128)(2,1)}, bf16[128,512]{1,0:T(8,128)(2,1)}, u32[]{:S(2)}, u32[]{:S(2)}) collective-permute-start(bf16[128,512]{1,0:T(8,128)(2,1)} %get-tuple-element.128), channel_id=1, source_target_pairs={{0,8},{8,0},{16,24},{24,16},{1,9},{9,1},{17,25},{25,17},{2,10},{10... | collective-permute-start | bytes 393224 | tf_op jit(solution)/shard_map/ppermute | solution.py:561
  161.7 13.1 %collective-permute-start.47 = (bf16[128,512]{1,0:T(8,128)(2,1)}, bf16[128,512]{1,0:T(8,128)(2,1)}, u32[]{:S(2)}, u32[]{:S(2)}) collective-permute-start(bf16[128,512]{1,0:T(8,128)(2,1)} %get-tuple-element.129), channel_id=1, source_target_pairs={{0,16},{8,24},{16,0},{24,8},{1,17},{9,25},{17,1},{25,9},{2,18},{10... | collective-permute-start | bytes 393224 | tf_op jit(solution)/shard_map/ppermute | solution.py:561
  164.7 10.1 %collective-permute-start.48 = (bf16[128,512]{1,0:T(8,128)(2,1)}, bf16[128,512]{1,0:T(8,128)(2,1)}, u32[]{:S(2)}, u32[]{:S(2)}) collective-permute-start(bf16[128,512]{1,0:T(8,128)(2,1)} %get-tuple-element.130), channel_id=1, source_target_pairs={{0,24},{8,16},{16,8},{24,0},{1,25},{9,17},{17,9},{25,1},{2,26},{10... | collective-permute-start | bytes 393224 | tf_op jit(solution)/shard_map/ppermute | solution.py:561
Sparse Core Ops, SparseCore 0:
  67.3 35.3 all-gather.2
